TPU v7x, 32 devices: a whole 2x2x4 slice. The times are simulated.
32 devices in a mesh: parts: 2 (over x), row: 16 (over z, y, core).
Axes of the slice: x: 2, y: 2, z: 4, core: 2. Of those that a mesh axis runs over, the one named last changes fastest.
Arguments:
- fitted: bfloat16 [64, 2048, 512], P(('parts', 'row')), parts along dimension 0, may hold values from -2 to 2
- fit_start: int32 [64], P('parts'), parts along dimension 0, may hold values from 0 to 1023
- virt_domain: int32 [64, 512], P('parts'), parts along dimension 0, may hold values from 0 to 255
- occ_energy: float32 [64], P('parts'), parts along dimension 0, may hold values from -2 to -0.5
- virt_energy: float32 [512], P('parts'), parts along dimension 0, may hold values from 0.2 to 3
- pair_partner: int32 [96], P('parts'), parts along dimension 0, may hold values from 0 to 31, as said below
Outputs:
- gradient: bfloat16 [64, 2048, 512], P(('parts', 'row')), parts along dimension 0
- density: float32 [64, 512, 512], P(('parts', 'row')), parts along dimension 0
There are 2 independent parts, one for each index of `parts`. A program takes and returns all parts, laid end to end along the dimension named above; each array names one. Nothing has to cross between parts.
Inputs may be any that keep to these rules, and one draw needn't show every extreme that they name: `pair_partner`: the second orbital of pair k lies between (k // 3 - 1) * 2 and (k // 3 + 2) * 2 - 1.
All inputs are finite; a program needn't handle non-finite values.
Results may differ from a plain program's by a relative error of at most 0.0056.
Values may be sent and summed in bfloat16 or wider, within the bound.
No kernel may reach another device: no remote copies, remote signals or barrier semaphores. Data moves between devices by JAX's collectives and lax.ppermute only.
A program may use at most 128 MiB of HBM per device.

v0:
```python
import jax
import jax.numpy as jnp
from jax import lax
from jax.sharding import PartitionSpec as P


def padded(cells, sides, width):
    for axis, dim in sides:
        count = lax.axis_size(axis)
        ends = count - 1
        head = lax.slice_in_dim(cells, 0, width, axis=dim)
        tail = lax.slice_in_dim(cells, cells.shape[dim] - width, cells.shape[dim], axis=dim)
        cells = jnp.concatenate(
            [
                lax.ppermute(tail, axis, [(i, (i + 1) % count) for i in range(ends)]),
                cells,
                lax.ppermute(head, axis, [((i + 1) % count, i) for i in range(ends)]),
            ],
            axis=dim,
        )
    return cells


def passed_along(array, axis, by):
    count = lax.axis_size(axis)
    pairs = [(i, i + by) for i in range(count) if 0 <= i + by < count]
    return lax.ppermute(array, axis, pairs)


def select_row(table, position):
    return lax.dynamic_index_in_dim(table, position, 0, keepdims=False)


def add_block(stack_all, position, value):
    return lax.dynamic_update_index_in_dim(
        stack_all, select_row(stack_all, position) + value, position, 0
    )


def shift_rows(fitted_block, from_start, to_start):
    row_shift = to_start - from_start
    row_count = fitted_block.shape[0]
    rolled = jnp.roll(fitted_block, -row_shift, axis=0)
    source = jnp.arange(row_count, dtype=jnp.int32) + row_shift
    inside = (source >= 0) & (source < row_count)
    return jnp.where(inside[:, None], rolled, jnp.zeros_like(rolled))


def amplitude_of(
    block_first,
    block_second,
    start_first,
    start_second,
    occ_first,
    occ_second,
    eps_first,
    eps_second,
):
    second_in_first = shift_rows(block_second, start_second, start_first)
    coulomb = lax.dot_general(
        block_first, second_in_first, (((0,), (0,)), ((), ())), preferred_element_type=jnp.float32
    )
    denominator = occ_first + occ_second - eps_first[:, None] - eps_second[None, :]
    return ((coulomb / denominator).astype(jnp.bfloat16), second_in_first)


def first_terms(amplitude, second_in_first, dens_scale):
    grad_first = lax.dot_general(
        second_in_first, amplitude, (((1,), (1,)), ((), ())), preferred_element_type=jnp.float32
    )
    dens_first = (
        lax.dot_general(
            amplitude, amplitude, (((1,), (1,)), ((), ())), preferred_element_type=jnp.float32
        )
        * dens_scale
    )
    return (grad_first, dens_first)


def second_terms(amplitude, block_first, start_first, start_second, dens_scale):
    first_in_second = shift_rows(block_first, start_first, start_second)
    grad_second = jnp.dot(first_in_second, amplitude, preferred_element_type=jnp.float32)
    dens_second = (
        lax.dot_general(
            amplitude, amplitude, (((0,), (0,)), ((), ())), preferred_element_type=jnp.float32
        )
        * dens_scale
    )
    return (grad_second, dens_second)


def on_device(fitted, fit_start, virt_domain, occ_energy, virt_energy, pair_partner):
    owned, aux_rows, virt_width = fitted.shape
    devices = lax.axis_size("row")
    pairs_here = pair_partner.shape[0] // devices
    dens_scale = float(virt_width) ** (-0.5)
    position = lax.axis_index("row")
    first_owned = position * owned
    wide = padded(fitted, (("row", 0),), owned)

    def orbital_data(orbital):
        return (
            select_row(fit_start, orbital),
            select_row(occ_energy, orbital),
            virt_energy[select_row(virt_domain, orbital)],
        )

    grad_terms = jnp.zeros((3 * owned, aux_rows, virt_width), jnp.float32)
    dens_terms = jnp.zeros((3 * owned, virt_width, virt_width), jnp.float32)
    for number in range(pairs_here):
        slot = owned + number % owned
        first_orb = first_owned + number % owned
        partner = select_row(pair_partner, position * pairs_here + number)
        place = partner - first_owned + owned
        start_first, occ_first, eps_first = orbital_data(first_orb)
        start_second, occ_second, eps_second = orbital_data(partner)
        block_first = wide[slot]
        amplitude, second_in_first = amplitude_of(
            block_first,
            select_row(wide, place),
            start_first,
            start_second,
            occ_first,
            occ_second,
            eps_first,
            eps_second,
        )
        grad_first, dens_first = first_terms(amplitude, second_in_first, dens_scale)
        grad_second, dens_second = second_terms(
            amplitude, block_first, start_first, start_second, dens_scale
        )
        grad_terms = add_block(add_block(grad_terms, slot, grad_first), place, grad_second)
        dens_terms = add_block(add_block(dens_terms, slot, dens_first), place, dens_second)
    grad_group = grad_terms.astype(jnp.bfloat16)
    dens_group = dens_terms.astype(jnp.bfloat16)
    from_after = passed_along((grad_group[:owned], dens_group[:owned]), "row", -1)
    from_before = passed_along((grad_group[2 * owned :], dens_group[2 * owned :]), "row", 1)
    grad_sum = (
        grad_group[owned : 2 * owned].astype(jnp.float32)
        + from_before[0].astype(jnp.float32)
        + from_after[0].astype(jnp.float32)
    )
    dens_sum = (
        dens_group[owned : 2 * owned].astype(jnp.float32)
        + from_before[1].astype(jnp.float32)
        + from_after[1].astype(jnp.float32)
    )
    return (grad_sum.astype(jnp.bfloat16), dens_sum)


def solution(mesh):
    placed = (
        P(("parts", "row"), None, None),
        P("parts"),
        P("parts", None),
        P("parts"),
        P("parts"),
        P("parts"),
    )
    return jax.shard_map(
        on_device,
        mesh=mesh,
        in_specs=placed,
        out_specs=(P(("parts", "row"), None, None), P(("parts", "row"), None, None)),
        check_vma=False,
    )
```

profile of v0, /device:TPU:19, one launch (start us, length us, event | category | flops | bytes accessed | tf_op | source)
XLA Modules:
  0.0 303.4 jit_solution(15098449269043019209)
XLA Ops:
  0.7 3.8 %collective-permute-start = (bf16[2,2048,512]{2,1,0:T(8,128)(2,1)}, bf16[2,2048,512]{2,1,0:T(8,128)(2,1)}, u32[]{:S(2)}, u32[]{:S(2)}) collective-permute-start(bf16[2,2048,512]{2,1,0:T(8,128)(2,1)} %param.8), channel_id=1, source_target_pairs={{0,1},{1,2},{2,3},{3,4},{4,5},{5,6},{6,7},{7,8},{8,9},{9,10},{10,1... | collective-permute-start | bytes 12582920 | tf_op jit(solution)/shard_map/ppermute | solution.py:15
  4.5 1.9 collective-permute-start.1
  25.5 3.5 %gather_fusion.1 = f32[512]{0:T(512)S(1)} fusion(f32[256]{0:T(256)S(1)} %copy-done, s32[1024]{0:T(1024)S(1)} %pad_clamp_fusion.3), kind=kCustom, calls=%fused_computation.1 | custom fusion | bytes 6144 | tf_op jit(solution)/shard_map/gather | solution.py:105
  29.0 3.5 %gather_fusion = f32[512]{0:T(512)S(1)} fusion(f32[256]{0:T(256)S(1)} %copy-done, s32[1024]{0:T(1024)S(1)} %get-tuple-element.39), kind=kCustom, calls=%fused_computation | custom fusion | bytes 6144 | tf_op jit(solution)/shard_map/gather | solution.py:105
  35.8 3.5 %gather_fusion.3 = f32[512]{0:T(512)S(1)} fusion(f32[256]{0:T(256)S(1)} %copy-done, s32[1024]{0:T(1024)S(1)} %get-tuple-element.37), kind=kCustom, calls=%fused_computation.3 | custom fusion | bytes 6144 | tf_op jit(solution)/shard_map/gather | solution.py:105
  39.3 3.5 %gather_fusion.2 = f32[512]{0:T(512)S(1)} fusion(f32[256]{0:T(256)S(1)} %copy-done, s32[1024]{0:T(1024)S(1)} %get-tuple-element.38), kind=kCustom, calls=%fused_computation.2 | custom fusion | bytes 6144 | tf_op jit(solution)/shard_map/gather | solution.py:105
  42.8 3.5 %gather_fusion.4 = f32[512]{0:T(512)S(1)} fusion(f32[256]{0:T(256)S(1)} %copy-done, s32[1024]{0:T(1024)S(1)} %get-tuple-element.36), kind=kCustom, calls=%fused_computation.4 | custom fusion | bytes 6144 | tf_op jit(solution)/shard_map/gather | solution.py:105
  47.8 4.5 %slice_bitcast_fusion.2 = (bf16[2048,512]{1,0:T(8,128)(2,1)}, bf16[2048,512]{1,0:T(8,128)(2,1)}) fusion(bf16[2,2048,512]{2,1,0:T(8,128)(2,1)} %param.8), kind=kLoop, calls=%fused_computation.51 | loop fusion | bytes 8388608 | tf_op jit(solution)/shard_map/squeeze | solution.py:117
  52.3 42.9 %collective-permute-done = bf16[2,2048,512]{2,1,0:T(8,128)(2,1)} collective-permute-done((bf16[2,2048,512]{2,1,0:T(8,128)(2,1)}, bf16[2,2048,512]{2,1,0:T(8,128)(2,1)}, u32[]{:S(2)}, u32[]{:S(2)}) %collective-permute-start) | collective-permute-done | bytes 4194336 | tf_op jit(solution)/shard_map/ppermute | solution.py:15
  95.2 2.5 constant_dynamic-update-slice_fusion.2
  98.2 2.7 constant_dynamic-update-slice_fusion
  102.7 3.3 %fusion.45 = bf16[512,512]{0,1:T(8,128)(2,1)S(1)} fusion(f32[512]{0:T(512)S(1)} %gather_fusion.1, f32[512]{0:T(512)S(1)} %get-tuple-element.18, bf16[2,2048,512]{2,1,0:T(8,128)(2,1)S(1)} %copy-done.2, s32[]{:T(128)S(6)} %select_n.196, bf16[2048,512]{1,0:T(8,128)(2,1)S(1)} %get-tuple-element.7, pred[2048]{0:T(1024)(128)(4,1)S(1)} %get-tuple-element.32), kind=kOutput, calls=%fused_computation.84 | convolution fusion | flops 1079771136 | bytes 4724740 | tf_op jit(solution)/shard_map/dot_general | solution.py:60
  106.0 4.6 %convolution_bitcast_fusion = f32[1,2048,512]{2,1,0:T(8,128)} fusion(bf16[512,512]{0,1:T(8,128)(2,1)S(1)} %fusion.45, s32[]{:T(128)S(6)} %select_n.196, bf16[2048,512]{1,0:T(8,128)(2,1)S(1)} %get-tuple-element.7, pred[2048]{0:T(1024)(128)(4,1)S(1)} %get-tuple-element.32), kind=kOutput, calls=%fused_computation.35 | convolution fusion | flops 1078984704 | bytes 6817796 | tf_op jit(solution)/shard_map/dot_general | solution.py:68
  110.6 13.6 %dynamic_update_slice.40 = f32[6,2048,512]{2,1,0:T(8,128)} pad(f32[1,2048,512]{2,1,0:T(8,128)} %convolution_bitcast_fusion, f32[]{:T(128)} %constant.171.clone.1), padding=2_3x0_0x0_0 | pad | bytes 29360132 | tf_op jit(solution)/shard_map/jit(dynamic_update_index_in_dim)/dynamic_update_slice | solution.py:35
  124.2 7.0 %fusion.3 = f32[6,2048,512]{2,1,0:T(8,128)} fusion(f32[6,2048,512]{2,1,0:T(8,128)} %dynamic_update_slice.40, s32[]{:T(128)S(6)} %select_n.166, f32[1,2048,512]{2,1,0:T(8,128)} %convolution_bitcast_fusion, bf16[512,512]{0,1:T(8,128)(2,1)S(1)} %fusion.45, s32[]{:T(128)S(6)} %select_n.198, bf16[2048,512]{1,0:T(8,128)(2,1)} %get-tuple-element.9, ...), kind=kOutput, calls=%fused_computation.14 | convolution fusion | flops 1080033280 | bytes 11012104 | tf_op jit(solution)/shard_map/dot_general | solution.py:82
  131.3 3.3 %fusion.47 = bf16[512,512]{0,1:T(8,128)(2,1)S(1)} fusion(f32[512]{0:T(512)S(1)} %gather_fusion.3, f32[512]{0:T(512)S(1)} %broadcast_subtract_fusion.1, bf16[2,2048,512]{2,1,0:T(8,128)(2,1)S(1)} %copy-done.3, s32[]{:T(128)S(6)} %select_n.200, bf16[2048,512]{1,0:T(8,128)(2,1)S(1)} %copy-done.4, pred[2048]{0:T(1024)(128)(4,1)S(1)} %get-tuple-element.34), kind=kOutput, calls=%fused_computation.86 | convolution fusion | flops 1079771136 | bytes 4724740 | tf_op jit(solution)/shard_map/dot_general | solution.py:60
  134.6 6.3 %fusion.9 = f32[6,2048,512]{2,1,0:T(8,128)} fusion(f32[6,2048,512]{2,1,0:T(8,128)} %fusion.3, bf16[512,512]{0,1:T(8,128)(2,1)S(1)} %fusion.47, s32[]{:T(128)S(6)} %select_n.200, bf16[2048,512]{1,0:T(8,128)(2,1)S(1)} %copy-done.4, pred[2048]{0:T(1024)(128)(4,1)S(1)} %get-tuple-element.34), kind=kOutput, calls=%fused_computation.22 | convolution fusion | flops 1080033280 | bytes 11012100 | tf_op jit(solution)/shard_map/dot_general | solution.py:68
  140.8 2.8 constant_dynamic-slice_fusion.4
  143.7 4.8 %bitcast_dynamic-update-slice_fusion.1 = f32[6,2048,512]{2,1,0:T(8,128)} fusion(f32[6,2048,512]{2,1,0:T(8,128)} %fusion.9, s32[]{:T(128)S(6)} %select_n.174, f32[1,2048,512]{2,1,0:T(8,128)S(1)} %constant_dynamic-slice_fusion.4, bf16[512,512]{0,1:T(8,128)(2,1)S(1)} %fusion.47, s32[]{:T(128)S(6)} %select_n.202, bf16[2048,512]{1,0:T(8,128)(2,1)S(1)} %copy-done.6, ...), kind=kOutput, calls=%fused_computation.33 | convolution fusion | flops 1080033280 | bytes 11012104 | tf_op jit(solution)/shard_map/dot_general | solution.py:82
  148.5 3.3 %fusion.49 = bf16[512,512]{0,1:T(8,128)(2,1)S(1)} fusion(f32[512]{0:T(512)S(1)} %gather_fusion.4, f32[512]{0:T(512)S(1)} %get-tuple-element.17, bf16[2,2048,512]{2,1,0:T(8,128)(2,1)S(1)} %copy-done.3, s32[]{:T(128)S(6)} %select_n.204, bf16[2048,512]{1,0:T(8,128)(2,1)S(1)} %get-tuple-element.5, pred[2048]{0:T(1024)(128)(4,1)S(1)} %fusion.73), kind=kOutput, calls=%fused_computation.88 | convolution fusion | flops 1079771136 | bytes 4724740 | tf_op jit(solution)/shard_map/dot_general | solution.py:60
  151.8 6.3 %fusion.6 = f32[6,2048,512]{2,1,0:T(8,128)} fusion(f32[6,2048,512]{2,1,0:T(8,128)} %bitcast_dynamic-update-slice_fusion.1, bf16[512,512]{0,1:T(8,128)(2,1)S(1)} %fusion.49, s32[]{:T(128)S(6)} %select_n.204, bf16[2048,512]{1,0:T(8,128)(2,1)S(1)} %get-tuple-element.5, pred[2048]{0:T(1024)(128)(4,1)S(1)} %fusion.73), kind=kOutput, calls=%fused_computation.18 | convolution fusion | flops 1080033280 | bytes 11012100 | tf_op jit(solution)/shard_map/dot_general | solution.py:68
  158.1 2.8 constant_dynamic-slice_fusion.2
  160.9 4.7 %bitcast_dynamic-update-slice_fusion = f32[6,2048,512]{2,1,0:T(8,128)} fusion(f32[6,2048,512]{2,1,0:T(8,128)} %fusion.6, s32[]{:T(128)S(6)} %select_n.181, f32[1,2048,512]{2,1,0:T(8,128)S(1)} %constant_dynamic-slice_fusion.2, bf16[512,512]{0,1:T(8,128)(2,1)S(1)} %fusion.49, s32[]{:T(128)S(6)} %select_n.206, bf16[2048,512]{1,0:T(8,128)(2,1)S(1)} %copy-done.5, ...), kind=kOutput, calls=%fused_computation.31 | convolution fusion | flops 1080033280 | bytes 11012104 | tf_op jit(solution)/shard_map/dot_general | solution.py:82
  165.6 9.2 %convert_element_type.39 = bf16[6,2048,512]{2,1,0:T(8,128)(2,1)S(1)} convert(f32[6,2048,512]{2,1,0:T(8,128)} %bitcast_dynamic-update-slice_fusion) | non-fusion elementwise | flops 6291456 | bytes 37748736 | tf_op jit(solution)/shard_map/convert_element_type | solution.py:134
  174.8 3.7 %fusion.92 = (bf16[2,2048,512]{2,1,0:T(8,128)(2,1)}, bf16[2,2048,512]{2,1,0:T(8,128)(2,1)}) fusion(bf16[6,2048,512]{2,1,0:T(8,128)(2,1)S(1)} %convert_element_type.39), kind=kLoop, calls=%fused_computation.158 | loop fusion | bytes 16777216 | tf_op jit(solution)/shard_map/slice | solution.py:137
  178.5 1.9 collective-permute-start.3
  180.4 4.3 %collective-permute-start.2 = (bf16[2,2048,512]{2,1,0:T(8,128)(2,1)}, bf16[2,2048,512]{2,1,0:T(8,128)(2,1)}, u32[]{:S(2)}, u32[]{:S(2)}) collective-permute-start(bf16[2,2048,512]{2,1,0:T(8,128)(2,1)} %get-tuple-element.3), channel_id=1, source_target_pairs={{0,1},{1,2},{2,3},{3,4},{4,5},{5,6},{6,7},{7,8},{8,9},{9,10},{10,1... | collective-permute-start | bytes 12582920 | tf_op jit(solution)/shard_map/ppermute | solution.py:27
  189.3 1.9 collective-permute-start.5
  191.2 3.6 %collective-permute-start.4 = (bf16[2,512,512]{2,1,0:T(8,128)(2,1)S(1)}, bf16[2,512,512]{2,1,0:T(8,128)(2,1)S(1)}, u32[]{:S(2)}, u32[]{:S(2)}) collective-permute-start(bf16[2,512,512]{2,1,0:T(8,128)(2,1)S(1)} %get-tuple-element.10), channel_id=1, source_target_pairs={{0,1},{1,2},{2,3},{3,4},{4,5},{5,6},{6,7},{7,8},{8,9},{9,10},{10,1... | collective-permute-start | bytes 3145736 | tf_op jit(solution)/shard_map/ppermute | solution.py:27
  194.9 101.7 %collective-permute-done.5 = bf16[2,512,512]{2,1,0:T(8,128)(2,1)S(1)} collective-permute-done((bf16[2,512,512]{2,1,0:T(8,128)(2,1)S(1)}, bf16[2,512,512]{2,1,0:T(8,128)(2,1)S(1)}, u32[]{:S(2)}, u32[]{:S(2)}) %collective-permute-start.5) | collective-permute-done | bytes 1048608 | tf_op jit(solution)/shard_map/ppermute | solution.py:27
  296.6 1.8 convert_add_fusion
  298.4 5.0 %add_convert_fusion = bf16[2,2048,512]{2,1,0:T(8,128)(2,1)} fusion(bf16[2,2048,512]{2,1,0:T(8,128)(2,1)S(1)} %collective-permute-done.3, bf16[2,2048,512]{2,1,0:T(8,128)(2,1)} %collective-permute-done.2, bf16[6,2048,512]{2,1,0:T(8,128)(2,1)S(1)} %convert_element_type.39), kind=kLoop, calls=%fused_computation.6 | loop fusion | flops 12582912 | bytes 16777216 | tf_op jit(solution)/shard_map/convert_element_type | solution.py:148
  (48 shorter events, 11.5 us)
Async XLA Ops:
  0.6 24.8 %copy-start = (f32[256]{0:T(256)S(1)}, f32[256]{0:T(256)}, u32[]{:S(2)}) copy-start(f32[256]{0:T(256)} %param.12) | copy-start | bytes 3076
  0.6 31.9 %copy-start.7 = (f32[32]{0:T(128)S(1)}, f32[32]{0:T(128)}, u32[]{:S(2)}) copy-start(f32[32]{0:T(128)} %param.11) | copy-start | bytes 388
  0.7 94.5 %collective-permute-start = (bf16[2,2048,512]{2,1,0:T(8,128)(2,1)}, bf16[2,2048,512]{2,1,0:T(8,128)(2,1)}, u32[]{:S(2)}, u32[]{:S(2)}) collective-permute-start(bf16[2,2048,512]{2,1,0:T(8,128)(2,1)} %param.8), channel_id=1, source_target_pairs={{0,1},{1,2},{2,3},{3,4},{4,5},{5,6},{6,7},{7,8},{8,9},{9,10},{10,1... | collective-permute-start | bytes 12582920 | tf_op jit(solution)/shard_map/ppermute | solution.py:15
  4.5 93.7 %collective-permute-start.1 = (bf16[2,2048,512]{2,1,0:T(8,128)(2,1)}, bf16[2,2048,512]{2,1,0:T(8,128)(2,1)}, u32[]{:S(2)}, u32[]{:S(2)}) collective-permute-start(bf16[2,2048,512]{2,1,0:T(8,128)(2,1)} %param.8), channel_id=1, source_target_pairs={{1,0},{2,1},{3,2},{4,3},{5,4},{6,5},{7,6},{8,7},{9,8},{10,9},{11,1... | collective-permute-start | bytes 12582920 | tf_op jit(solution)/shard_map/ppermute | solution.py:17
  52.3 45.3 %copy-start.2 = (bf16[2,2048,512]{2,1,0:T(8,128)(2,1)S(1)}, bf16[2,2048,512]{2,1,0:T(8,128)(2,1)}, u32[]{:S(2)}) copy-start(bf16[2,2048,512]{2,1,0:T(8,128)(2,1)} %param.8) | copy-start | bytes 12582916
  124.2 7.0 %copy-start.3 = (bf16[2,2048,512]{2,1,0:T(8,128)(2,1)S(1)}, bf16[2,2048,512]{2,1,0:T(8,128)(2,1)}, u32[]{:S(2)}) copy-start(bf16[2,2048,512]{2,1,0:T(8,128)(2,1)} %param.8) | copy-start | bytes 12582916
  124.2 7.0 %copy-start.4 = (bf16[2048,512]{1,0:T(8,128)(2,1)S(1)}, bf16[2048,512]{1,0:T(8,128)(2,1)}, u32[]{:S(2)}) copy-start(bf16[2048,512]{1,0:T(8,128)(2,1)} %get-tuple-element.6) | copy-start | bytes 6291460
  140.8 2.9 copy-start.6
  158.1 2.9 copy-start.5
  178.5 119.8 %collective-permute-start.3 = (bf16[2,2048,512]{2,1,0:T(8,128)(2,1)}, bf16[2,2048,512]{2,1,0:T(8,128)(2,1)S(1)}, u32[]{:S(2)}, u32[]{:S(2)}) collective-permute-start(bf16[2,2048,512]{2,1,0:T(8,128)(2,1)} %get-tuple-element.4), channel_id=1, source_target_pairs={{1,0},{2,1},{3,2},{4,3},{5,4},{6,5},{7,6},{8,7},{9,8},{10,9},{11,1... | collective-permute-start | bytes 12582920 | tf_op jit(solution)/shard_map/ppermute | solution.py:27
  180.4 117.9 %collective-permute-start.2 = (bf16[2,2048,512]{2,1,0:T(8,128)(2,1)}, bf16[2,2048,512]{2,1,0:T(8,128)(2,1)}, u32[]{:S(2)}, u32[]{:S(2)}) collective-permute-start(bf16[2,2048,512]{2,1,0:T(8,128)(2,1)} %get-tuple-element.3), channel_id=1, source_target_pairs={{0,1},{1,2},{2,3},{3,4},{4,5},{5,6},{6,7},{7,8},{8,9},{9,10},{10,1... | collective-permute-start | bytes 12582920 | tf_op jit(solution)/shard_map/ppermute | solution.py:27
  189.3 107.3 %collective-permute-start.5 = (bf16[2,512,512]{2,1,0:T(8,128)(2,1)S(1)}, bf16[2,512,512]{2,1,0:T(8,128)(2,1)S(1)}, u32[]{:S(2)}, u32[]{:S(2)}) collective-permute-start(bf16[2,512,512]{2,1,0:T(8,128)(2,1)S(1)} %get-tuple-element.11), channel_id=1, source_target_pairs={{1,0},{2,1},{3,2},{4,3},{5,4},{6,5},{7,6},{8,7},{9,8},{10,9},{11,1... | collective-permute-start | bytes 3145736 | tf_op jit(solution)/shard_map/ppermute | solution.py:27
  191.2 105.4 %collective-permute-start.4 = (bf16[2,512,512]{2,1,0:T(8,128)(2,1)S(1)}, bf16[2,512,512]{2,1,0:T(8,128)(2,1)S(1)}, u32[]{:S(2)}, u32[]{:S(2)}) collective-permute-start(bf16[2,512,512]{2,1,0:T(8,128)(2,1)S(1)} %get-tuple-element.10), channel_id=1, source_target_pairs={{0,1},{1,2},{2,3},{3,4},{4,5},{5,6},{6,7},{7,8},{8,9},{9,10},{10,1... | collective-permute-start | bytes 3145736 | tf_op jit(solution)/shard_map/ppermute | solution.py:27
  298.4 5.0 %copy-start.1 = (f32[256]{0:T(256)S(1)}, f32[256]{0:T(256)}, u32[]{:S(2)}) copy-start(f32[256]{0:T(256)} %param.12) | copy-start | bytes 3076
where the time goes:
time: 304 us; the launch traced here: 303 us
  waiting for transfers between devices  145 us (48%)
  local copies, waits for them, and re-layouts  57.4 us (19%)
  matrix products  46.4 us (15%)
  between operations  20.1 us (7%)
  starting transfers between devices  17.5 us (6%)
  other arithmetic  17.4 us (6%)
    ppermute x4, waiting for transfers between devices, passed_along(): return lax.ppermute(array, axis, pairs)  102 us
    ppermute x1, waiting for transfers between devices, padded(): lax.ppermute(tail, axis, [(i, (i + 1) % count) for i in range(ends)])  42.9 us
    gather x5, local copies, waits for them, and re-layouts, orbital_data(): virt_energy[select_row(virt_domain, orbital)]  17.6 us
    dot_general x3, matrix products, first_terms(): lax.dot_general(second_in_first, amplitude, (((1,), (1,)), ((), ())), pre...  17.1 us
    dot_general x3, matrix products, second_terms(): jnp.dot(first_in_second, amplitude, preferred_element_type=jnp.float32)  16.5 us
    dynamic_update_slice x2, local copies, waits for them, and re-layouts, add_block(): lax.dynamic_update_index_in_dim(stack_all, select_row(stack_all, position...  14.4 us
    ppermute x4, starting transfers between devices, passed_along(): return lax.ppermute(array, axis, pairs)  11.8 us
    dot_general x3, matrix products, amplitude_of(): lax.dot_general(block_first, second_in_first, (((0,), (0,)), ((), ())), p...  9.94 us
  transfers between devices with their start and end apart: 6, of which 2 were waited for; matrix products, arithmetic and copies ran while one was open for 12% of the time, Pallas kernels for 0%

commit v1 on v0

v1 whole, which is shorter than its diff:
```python
import functools

import jax
import jax.numpy as jnp
from jax import lax
from jax.experimental import pallas as pl
from jax.experimental.pallas import tpu as pltpu
from jax.sharding import PartitionSpec as P

SUB = 16
LANES = 128
COLS = 256
REACH = 1024
VMEM_BYTES = 50 * 1024 * 1024
NT = (((1,), (1,)), ((), ()))


def dot_nt(a, b):
    return lax.dot_general(a, b, NT, preferred_element_type=jnp.float32)


def up_to(value, unit):
    return -(-value // unit) * unit


def clear_margins(buf, rows):
    buf[:REACH, :] = jnp.zeros((REACH, buf.shape[1]), buf.dtype)
    tail = buf.shape[0] - REACH - rows
    buf[REACH + rows :, :] = jnp.zeros((tail, buf.shape[1]), buf.dtype)


def slot_of(owned, group, s, t):
    return (group * owned + s) * owned + t


def amplitude_of(meta, shifted, group, s, t, h, eps_col, eps_row, ft):
    coulomb = jnp.dot(ft[s], shifted, preferred_element_type=jnp.float32)
    denominator = meta - eps_col[s] - eps_row[group, t, h]
    return (coulomb / denominator).astype(jnp.bfloat16)


def add_rows(acc, s, buf, offset, amplitude, weight, rows, step):
    def one(i, carry):
        base = pl.multiple_of(i * step, step)
        block = buf[pl.ds(pl.multiple_of(offset + base, SUB), step), :]
        acc[s, pl.ds(base, step), :] += weight * dot_nt(block, amplitude)
        return carry

    whole = rows // step
    lax.fori_loop(0, whole, one, 0)
    rest = rows - whole * step
    if rest:
        base = whole * step
        block = buf[pl.ds(pl.multiple_of(offset + base, SUB), rest), :]
        acc[s, base:rows, :] += weight * dot_nt(block, amplitude)


def gather_block(count, shift, occ, group, t, h, eps_col, eps_row, ft, buf, acc, dens):
    owned, rows, width = acc.shape
    depth = ft.shape[2]
    scale = float(width) ** -0.5

    def one(s, carry):
        slot = slot_of(owned, group, s, t)

        @pl.when(count[slot] != 0)
        def _():
            weight = count[slot].astype(jnp.float32)
            offset = pl.multiple_of(REACH + shift[slot], SUB)
            amplitude = amplitude_of(
                occ[slot], buf[pl.ds(offset, depth), :], group, s, t, h, eps_col, eps_row, ft
            )
            dens[s] += (weight * scale) * dot_nt(amplitude, amplitude)
            add_rows(acc, s, buf, offset, amplitude, weight, rows, 256)

        return carry

    lax.fori_loop(0, owned, one, 0)


def near_kernel(
    count, shift, occ, eps_col, eps_row, own, mate, acc, dens, ft, buf, *, halves
):
    rows = own.shape[1]
    depth = ft.shape[2]
    clear_margins(buf, rows)
    acc[...] = jnp.zeros_like(acc)
    dens[...] = jnp.zeros_like(dens)

    def turn(j, carry):
        buf[REACH : REACH + rows, :] = own[j]

        def tile(i, inner):
            at = pl.multiple_of(i * LANES, LANES)
            block = buf[pl.ds(REACH + at, LANES), :]
            ft[
                j // halves, pl.ds(pl.multiple_of((j % halves) * COLS, COLS), COLS), pl.ds(at, LANES)
            ] = block.T
            return inner

        return lax.fori_loop(0, depth // LANES, tile, carry)

    lax.fori_loop(0, own.shape[0], turn, 0)

    for group, stack in ((0, own), (1, mate)):

        def one(j, carry):
            buf[REACH : REACH + rows, :] = stack[j]
            gather_block(
                count, shift, occ, group, j // halves, j % halves,
                eps_col, eps_row, ft, buf, acc, dens,
            )
            return carry

        lax.fori_loop(0, stack.shape[0], one, 0)


def far_kernel(
    count, shift, occ, eps_col, eps_row, ft, acc_in, dens_in, *refs, halves
):
    *blocks, acc, dens, buf, sem = refs
    rows = blocks[0].shape[0]
    load_acc = pltpu.make_async_copy(acc_in, acc, sem.at[0])
    load_dens = pltpu.make_async_copy(dens_in, dens, sem.at[1])
    load_acc.start()
    load_dens.start()
    clear_margins(buf, rows)
    load_acc.wait()
    load_dens.wait()
    for j, block in enumerate(blocks):
        buf[REACH : REACH + rows, :] = block[...]
        gather_block(
            count, shift, occ, 2, j // halves, j % halves,
            eps_col, eps_row, ft, buf, acc, dens,
        )


def last_kernel(
    count, shift, occ, lead, eps_col, eps_row, ft_in, block, acc_in, dens_in,
    out, dens, buf, ft, acc, amp, sem, *, t, h,
):
    owned, rows, width = acc_in.shape
    depth = ft.shape[2]
    scale = float(width) ** -0.5
    out_rows = out.shape[1]
    load_block = pltpu.make_async_copy(block, buf.at[pl.ds(REACH, rows)], sem.at[0])
    load_block.start()
    load_ft, load_acc = [], []
    for s in range(owned):
        load_ft.append(pltpu.make_async_copy(ft_in.at[s], ft.at[s], sem.at[2 + s]))
        load_ft[s].start()
    for s in range(owned):
        load_acc.append(
            pltpu.make_async_copy(acc_in.at[s], acc.at[s, pl.ds(0, rows)], sem.at[2 + owned + s])
        )
        load_acc[s].start()
    load_dens = pltpu.make_async_copy(dens_in, dens, sem.at[1])
    load_dens.start()
    clear_margins(buf, rows)
    load_block.wait()
    for s in range(owned):
        load_ft[s].wait()
        slot = slot_of(owned, 2, s, t)

        @pl.when(count[slot] != 0)
        def _():
            offset = pl.multiple_of(REACH + shift[slot], SUB)
            amp[s] = amplitude_of(
                occ[slot], buf[pl.ds(offset, depth), :], 2, s, t, h, eps_col, eps_row, ft
            )

    load_dens.wait()
    for s in range(owned):
        load_acc[s].wait()
        slot = slot_of(owned, 2, s, t)

        @pl.when(count[slot] != 0)
        def _():
            weight = count[slot].astype(jnp.float32)
            offset = pl.multiple_of(REACH + shift[slot], SUB)
            amplitude = amp[s]
            dens[s] += (weight * scale) * dot_nt(amplitude, amplitude)
            add_rows(acc, s, buf, offset, amplitude, weight, rows, 256)

        def settle(i, carry):
            base = pl.multiple_of(i * LANES, LANES)
            skip = lead[s] % 8
            start = pl.multiple_of(base + (lead[s] - skip), 8)
            taken = LANES + 8
            block = pltpu.roll(acc[s, pl.ds(start, taken), :], (taken - skip) % taken, 0)
            out[s, pl.ds(base, LANES), :] = block[:LANES].astype(out.dtype)
            return carry

        lax.fori_loop(0, out_rows // LANES, settle, 0)


def spec(space):
    return pl.BlockSpec(memory_space=space)


def on_device(fitted, fit_start, virt_domain, occ_energy, virt_energy, pair_partner):
    owned, aux, width = fitted.shape
    devices = lax.axis_size("row")
    position = lax.axis_index("row")
    orbitals = fit_start.shape[0]
    pairs = pair_partner.shape[0]
    pairs_here = pairs // devices
    halves = width // COLS
    rows = aux + SUB
    depth = up_to(rows, LANES)
    buf_rows = 2 * REACH + depth

    own_start = lax.dynamic_slice_in_dim(fit_start, position * owned, owned, 0)
    lead = own_start % SUB
    chunks = []
    for t in range(owned):
        for h in range(halves):
            piece = fitted[t, :, h * COLS : (h + 1) * COLS]
            empty = jnp.zeros((rows, COLS), fitted.dtype)
            chunks.append(lax.dynamic_update_slice(empty, piece, (lead[t], 0)))

    outward = []
    for i in range(devices):
        to = i + 1 if i % 2 else i - 1
        if 0 <= to < devices:
            outward.append((i, to))
    inward = [(i, i ^ 1) for i in range(devices) if i ^ 1 < devices]
    far = [lax.ppermute(chunk, "row", outward) for chunk in chunks]
    own = jnp.stack(chunks)
    mate = lax.ppermute(own, "row", inward)

    side = jnp.where(position % 2 == 1, 1, -1)
    bases = jnp.stack([position, position - side, position + side]) * owned
    places = bases[:, None] + jnp.arange(owned, dtype=jnp.int32)
    inside = jnp.clip(places, 0, orbitals - 1)
    pick = inside[:, :, None] == jnp.arange(orbitals, dtype=jnp.int32)
    starts = jnp.sum(jnp.where(pick, fit_start, 0), axis=-1)
    occs = jnp.sum(jnp.where(pick, occ_energy, 0.0), axis=-1)
    aligned = starts - starts % SUB
    mine = places[0]
    shift = aligned[0][None, :, None] - aligned[:, None, :]
    occ = occs[0][None, :, None] + occs[:, None, :]
    ordinal = jnp.arange(pairs, dtype=jnp.int32)
    first = (ordinal // pairs_here) * owned + (ordinal % pairs_here) % owned
    is_mine = mine[None, :, None, None]
    is_other = places[:, None, :, None]
    count = jnp.sum(
        ((first == is_mine) & (pair_partner == is_other)).astype(jnp.int32)
        + ((pair_partner == is_mine) & (first == is_other)).astype(jnp.int32),
        axis=-1,
    )
    domains = jnp.stack(
        [lax.dynamic_slice_in_dim(virt_domain, bases[g], owned, 0) for g in range(3)]
    )
    table = jnp.arange(virt_energy.shape[0], dtype=jnp.int32)
    eps = jnp.sum(jnp.where(domains[..., None] == table, virt_energy, 0.0), axis=-1)
    eps_col = eps[0].reshape(owned, width, 1)
    eps_row = eps.reshape(3, owned, halves, 1, COLS)
    count, shift, occ = count.reshape(-1), shift.reshape(-1), occ.reshape(-1)

    smem, vmem, anywhere = spec(pltpu.SMEM), spec(pltpu.VMEM), spec(pl.ANY)
    params = pltpu.CompilerParams(vmem_limit_bytes=VMEM_BYTES)
    unit = 2 * rows * width * COLS * 2
    f32_acc = jax.ShapeDtypeStruct((owned, rows, width), jnp.float32)
    f32_dens = jax.ShapeDtypeStruct((owned, width, width), jnp.float32)
    ft_shape = jax.ShapeDtypeStruct((owned, width, depth), fitted.dtype)
    buf = pltpu.VMEM((buf_rows, COLS), fitted.dtype)

    acc, dens, ft = pl.pallas_call(
        functools.partial(near_kernel, halves=halves),
        out_shape=(f32_acc, f32_dens, ft_shape),
        in_specs=[smem] * 3 + [vmem] * 4,
        out_specs=(vmem, vmem, vmem),
        scratch_shapes=[buf],
        compiler_params=params,
        cost_estimate=pl.CostEstimate(
            flops=unit * 2 * owned * owned * halves, bytes_accessed=24 << 20, transcendentals=0
        ),
        name="near_pairs",
    )(count, shift, occ, eps_col, eps_row, own, mate)

    acc, dens = pl.pallas_call(
        functools.partial(far_kernel, halves=halves),
        out_shape=(f32_acc, f32_dens),
        in_specs=[smem] * 3 + [vmem] * 3 + [anywhere] * 2 + [vmem] * (len(far) - 1),
        out_specs=(vmem, vmem),
        scratch_shapes=[buf, pltpu.SemaphoreType.DMA((2,))],
        compiler_params=params,
        cost_estimate=pl.CostEstimate(
            flops=unit * owned * (len(far) - 1), bytes_accessed=28 << 20, transcendentals=0
        ),
        name="far_pairs",
    )(count, shift, occ, eps_col, eps_row, ft, acc, dens, *far[:-1])

    gradient, density = pl.pallas_call(
        functools.partial(last_kernel, t=(len(far) - 1) // halves, h=(len(far) - 1) % halves),
        out_shape=(
            jax.ShapeDtypeStruct(fitted.shape, fitted.dtype),
            f32_dens,
        ),
        in_specs=[smem] * 4 + [vmem] * 2 + [anywhere] * 4,
        out_specs=(vmem, vmem),
        scratch_shapes=[
            buf,
            pltpu.VMEM(ft_shape.shape, ft_shape.dtype),
            pltpu.VMEM((owned, depth, width), jnp.float32),
            pltpu.VMEM((owned, width, COLS), jnp.bfloat16),
            pltpu.SemaphoreType.DMA((2 + 2 * owned,)),
        ],
        compiler_params=params,
        cost_estimate=pl.CostEstimate(
            flops=unit * owned, bytes_accessed=20 << 20, transcendentals=0
        ),
        name="last_pairs",
    )(count, shift, occ, lead, eps_col, eps_row, ft, far[-1], acc, dens)
    return gradient, density


def solution(mesh):
    placed = (
        P(("parts", "row"), None, None),
        P("parts"),
        P("parts", None),
        P("parts"),
        P("parts"),
        P("parts"),
    )
    return jax.shard_map(
        on_device,
        mesh=mesh,
        in_specs=placed,
        out_specs=(P(("parts", "row"), None, None), P(("parts", "row"), None, None)),
        check_vma=False,
    )
```

time: 304 us -> 182 us (0.60)
  the two profiles are of different devices: /device:TPU:19 before, /device:TPU:25 now
where the time goes in v1:
time: 182 us; the launch traced here: 181 us
  Pallas kernels  76.8 us (42%)
  waiting for transfers between devices  37.7 us (21%)
  local copies, waits for them, and re-layouts  37.2 us (20%)
  starting transfers between devices  11.8 us (6%)
  between operations  10.6 us (6%)
  other arithmetic  6.64 us (4%)
    ppermute x4, waiting for transfers between devices, on_device(): far = [lax.ppermute(chunk, 'row', outward) for chunk in chunks]  37.7 us
    pallas_call x1, Pallas kernels, on_device(): pl.pallas_call(functools.partial(near_kernel, halves=halves), out_shape=(...  35.6 us
    pallas_call x1, Pallas kernels, on_device(): pl.pallas_call(functools.partial(far_kernel, halves=halves), out_shape=(f...  28.7 us
    dynamic_update_slice x4, local copies, waits for them, and re-layouts, on_device(): chunks.append(lax.dynamic_update_slice(empty, piece, (lead[t], 0)))  23.9 us
    pallas_call x1, Pallas kernels, on_device(): pl.pallas_call(functools.partial(last_kernel, t=(len(far) - 1) // halves,...  12.5 us
    ppermute x4, starting transfers between devices, on_device(): far = [lax.ppermute(chunk, 'row', outward) for chunk in chunks]  11.1 us
    another operation x4, local copies, waits for them, and re-layouts  4.29 us
    another operation x1, other arithmetic, on_device(): own = jnp.stack(chunks)  3.81 us
  transfers between devices with their start and end apart: 5, of which 3 were waited for; matrix products, arithmetic and copies ran while one was open for 2% of the time, Pallas kernels for 36%

profile of v1, /device:TPU:25, one launch (start us, length us, event | category | flops | bytes accessed | tf_op | source)
XLA Modules:
  0.0 180.7 jit_solution(5256854256538155449)
XLA Ops:
  0.6 0.7 and_select_fusion.lead
  1.4 0.7 fusion.8
  4.7 3.4 %slice_bitcast_fusion.3 = (bf16[2048,256]{1,0:T(8,128)(2,1)S(1)}, bf16[2048,256]{1,0:T(8,128)(2,1)S(1)}, bf16[2048,256]{1,0:T(8,128)(2,1)S(1)}, bf16[2048,256]{1,0:T(8,128)(2,1)}) fusion(bf16[2,2048,512]{2,1,0:T(8,128)(2,1)} %param.6), kind=kLoop, calls=%fused_computation.6 | loop fusion | bytes 8388608 | tf_op jit(solution)/shard_map/squeeze | solution.py:218
  9.4 1.0 broadcast.203.clone.1
  10.5 6.2 %dynamic_update_slice.14 = bf16[2064,256]{1,0:T(8,128)(2,1)} dynamic-update-slice(bf16[2064,256]{1,0:T(8,128)(2,1)} %broadcast.203.clone.1, bf16[2048,256]{1,0:T(8,128)(2,1)} %get-tuple-element.15, s32[]{:T(128)S(6)} %select_n.104, s32[]{:T(128)} %constant.68.clone.1) | dynamic-update-slice | bytes 2097156 | tf_op jit(solution)/shard_map/dynamic_update_slice | solution.py:220
  16.6 1.0 broadcast.203.clone
  17.7 5.9 %dynamic_update_slice.15 = bf16[2064,256]{1,0:T(8,128)(2,1)} dynamic-update-slice(bf16[2064,256]{1,0:T(8,128)(2,1)} %broadcast.203.clone, bf16[2048,256]{1,0:T(8,128)(2,1)S(1)} %get-tuple-element.14, s32[]{:T(128)S(6)} %select_n.104, s32[]{:T(128)} %constant.68.clone.1) | dynamic-update-slice | bytes 2097156 | tf_op jit(solution)/shard_map/dynamic_update_slice | solution.py:220
  23.6 1.1 broadcast.203.clone.3
  24.7 5.9 %dynamic_update_slice.12 = bf16[2064,256]{1,0:T(8,128)(2,1)} dynamic-update-slice(bf16[2064,256]{1,0:T(8,128)(2,1)} %broadcast.203.clone.3, bf16[2048,256]{1,0:T(8,128)(2,1)S(1)} %get-tuple-element.12, s32[]{:T(128)S(6)} %select_n.103, s32[]{:T(128)} %constant.68.clone.1) | dynamic-update-slice | bytes 2097156 | tf_op jit(solution)/shard_map/dynamic_update_slice | solution.py:220
  30.5 1.1 broadcast.203.clone.2
  31.7 5.9 %dynamic_update_slice.13 = bf16[2064,256]{1,0:T(8,128)(2,1)} dynamic-update-slice(bf16[2064,256]{1,0:T(8,128)(2,1)} %broadcast.203.clone.2, bf16[2048,256]{1,0:T(8,128)(2,1)S(1)} %get-tuple-element.13, s32[]{:T(128)S(6)} %select_n.103, s32[]{:T(128)} %constant.68.clone.1) | dynamic-update-slice | bytes 2097156 | tf_op jit(solution)/shard_map/dynamic_update_slice | solution.py:220
  37.6 3.8 %pad_maximum_fusion.own = bf16[4,2064,256]{2,1,0:T(8,128)(2,1)} fusion(bf16[1,2064,256]{2,1,0:T(8,128)(2,1)} %bitcast.22, bf16[1,2064,256]{2,1,0:T(8,128)(2,1)} %bitcast.20, bf16[1,2064,256]{2,1,0:T(8,128)(2,1)} %bitcast.17, bf16[1,2064,256]{2,1,0:T(8,128)(2,1)} %bitcast.15), kind=kLoop, calls=%fused_computation | loop fusion | flops 6340608 | bytes 8454144 | tf_op jit(solution)/shard_map/stack | solution.py:229
  41.4 0.7 collective-permute-start
  42.1 3.0 %collective-permute-start.3 = (bf16[2064,256]{1,0:T(8,128)(2,1)}, bf16[2064,256]{1,0:T(8,128)(2,1)S(1)}, u32[]{:S(2)}, u32[]{:S(2)}) collective-permute-start(bf16[2064,256]{1,0:T(8,128)(2,1)} %dynamic_update_slice.13), channel_id=1, source_target_pairs={{1,2},{2,1},{3,4},{4,3},{5,6},{6,5},{7,8},{8,7},{9,10},{10,9},{11,... | collective-permute-start | bytes 3170312 | tf_op jit(solution)/shard_map/ppermute | solution.py:228
  45.1 2.6 %collective-permute-start.2 = (bf16[2064,256]{1,0:T(8,128)(2,1)}, bf16[2064,256]{1,0:T(8,128)(2,1)}, u32[]{:S(2)}, u32[]{:S(2)}) collective-permute-start(bf16[2064,256]{1,0:T(8,128)(2,1)} %dynamic_update_slice.12), channel_id=1, source_target_pairs={{1,2},{2,1},{3,4},{4,3},{5,6},{6,5},{7,8},{8,7},{9,10},{10,9},{11,... | collective-permute-start | bytes 3170312 | tf_op jit(solution)/shard_map/ppermute | solution.py:228
  47.7 3.0 %collective-permute-start.1 = (bf16[2064,256]{1,0:T(8,128)(2,1)}, bf16[2064,256]{1,0:T(8,128)(2,1)S(1)}, u32[]{:S(2)}, u32[]{:S(2)}) collective-permute-start(bf16[2064,256]{1,0:T(8,128)(2,1)} %dynamic_update_slice.15), channel_id=1, source_target_pairs={{1,2},{2,1},{3,4},{4,3},{5,6},{6,5},{7,8},{8,7},{9,10},{10,9},{11,... | collective-permute-start | bytes 3170312 | tf_op jit(solution)/shard_map/ppermute | solution.py:228
  50.7 2.6 %collective-permute-start.4 = (bf16[2064,256]{1,0:T(8,128)(2,1)}, bf16[2064,256]{1,0:T(8,128)(2,1)}, u32[]{:S(2)}, u32[]{:S(2)}) collective-permute-start(bf16[2064,256]{1,0:T(8,128)(2,1)} %dynamic_update_slice.14), channel_id=1, source_target_pairs={{1,2},{2,1},{3,4},{4,3},{5,6},{6,5},{7,8},{8,7},{9,10},{10,9},{11,... | collective-permute-start | bytes 3170312 | tf_op jit(solution)/shard_map/ppermute | solution.py:228
  53.4 0.7 fusion.9
  58.2 0.2 fusion.1
  58.5 0.2 select_reduce_fusion.2
  58.9 0.2 select_reduce_fusion.1
  61.1 0.8 dynamic-slice_bitcast_fusion.2
  62.0 1.0 select_reduce_fusion
  63.1 0.2 copy.13.eps_col
  63.3 35.6 %near_pairs.1 = (f32[2,2064,512]{2,1,0:T(8,128)}, f32[2,512,512]{2,1,0:T(8,128)S(1)}, bf16[2,512,2176]{2,1,0:T(8,128)(2,1)}) custom-call(s32[12]{0:T(128)S(1)} %reshape.171.count, s32[12]{0:T(128)S(1)} %sub.44.shift, f32[12]{0:T(128)S(1)} %add.132.occ, f32[2,512,1]{2,1,0:T(8,128)S(1)} %copy.13.eps_col, f32[3,2,2,1,256]{4,3,2,1,0:T(1,128)S(1)} %reshape.172.eps_row, ...), custom_call_target="tpu_custom_call" | custom-call | flops 17314086912 | bytes 25165824 | tf_op jit(solution)/shard_map/near_pairs/pallas_call | solution.py:269
  98.9 1.3 copy-done.1
  100.2 3.6 %collective-permute-done.3.refs_1_ = bf16[2064,256]{1,0:T(8,128)(2,1)S(1)} collective-permute-done((bf16[2064,256]{1,0:T(8,128)(2,1)}, bf16[2064,256]{1,0:T(8,128)(2,1)S(1)}, u32[]{:S(2)}, u32[]{:S(2)}) %collective-permute-start.3) | collective-permute-done | bytes 1056800 | tf_op jit(solution)/shard_map/ppermute | solution.py:228
  103.8 11.4 %collective-permute-done.2.refs_0_ = bf16[2064,256]{1,0:T(8,128)(2,1)} collective-permute-done((bf16[2064,256]{1,0:T(8,128)(2,1)}, bf16[2064,256]{1,0:T(8,128)(2,1)}, u32[]{:S(2)}, u32[]{:S(2)}) %collective-permute-start.2) | collective-permute-done | bytes 1056800 | tf_op jit(solution)/shard_map/ppermute | solution.py:228
  115.3 22.6 %collective-permute-done.4.refs_2_ = bf16[2064,256]{1,0:T(8,128)(2,1)} collective-permute-done((bf16[2064,256]{1,0:T(8,128)(2,1)}, bf16[2064,256]{1,0:T(8,128)(2,1)}, u32[]{:S(2)}, u32[]{:S(2)}) %collective-permute-start.4) | collective-permute-done | bytes 1056800 | tf_op jit(solution)/shard_map/ppermute | solution.py:228
  137.9 28.7 %far_pairs.1 = (f32[2,2064,512]{2,1,0:T(8,128)}, f32[2,512,512]{2,1,0:T(8,128)}) custom-call(s32[12]{0:T(128)S(1)} %reshape.171.count, s32[12]{0:T(128)S(1)} %sub.44.shift, f32[12]{0:T(128)S(1)} %add.132.occ, f32[2,512,1]{2,1,0:T(8,128)S(1)} %copy.13.eps_col, f32[3,2,2,1,256]{4,3,2,1,0:T(1,128)S(1)} %reshape.172.eps_row, ...), custom_call_target="tpu_custom_call" | custom-call | flops 6492782592 | bytes 29360128 | tf_op jit(solution)/shard_map/far_pairs/pallas_call | solution.py:282
  166.6 1.6 copy-done
  168.2 12.5 %last_pairs.1 = (bf16[2,2048,512]{2,1,0:T(8,128)(2,1)}, f32[2,512,512]{2,1,0:T(8,128)}) custom-call(s32[12]{0:T(128)S(1)} %reshape.171.count, s32[12]{0:T(128)S(1)} %sub.44.shift, f32[12]{0:T(128)S(1)} %add.132.occ, s32[2]{0:T(128)S(1)} %and_select_fusion.lead, f32[2,512,1]{2,1,0:T(8,128)S(1)} %copy.13.eps_col, f32[3,2,2,1,256]{4,3,2,1,0:T(1,128)S(1)} %reshape.172.eps_row, ...), custom_call_target="tpu_custom_call" | custom-call | flops 2164260864 | bytes 20971520 | tf_op jit(solution)/shard_map/last_pairs/pallas_call | solution.py:295
  (29 shorter events, 0.8 us)
Async XLA Ops:
  37.6 20.4 %copy-start.2 = (s32[48]{0:T(128)S(1)}, s32[48]{0:T(128)}, u32[]{:S(2)}) copy-start(s32[48]{0:T(128)} %param.11) | copy-start | bytes 580
  37.6 20.8 %copy-start.4 = (s32[32]{0:T(128)S(1)}, s32[32]{0:T(128)}, u32[]{:S(2)}) copy-start(s32[32]{0:T(128)} %param.7) | copy-start | bytes 388
  37.6 21.2 %copy-start.5 = (f32[32]{0:T(128)S(1)}, f32[32]{0:T(128)}, u32[]{:S(2)}) copy-start(f32[32]{0:T(128)} %param.9) | copy-start | bytes 388
  37.6 24.4 %copy-start.3 = (f32[256]{0:T(256)S(1)}, f32[256]{0:T(256)}, u32[]{:S(2)}) copy-start(f32[256]{0:T(256)} %param.10) | copy-start | bytes 3076
  41.4 21.9 %collective-permute-start = (bf16[4,2064,256]{2,1,0:T(8,128)(2,1)}, bf16[4,2064,256]{2,1,0:T(8,128)(2,1)}, u32[]{:S(2)}, u32[]{:S(2)}) collective-permute-start(bf16[4,2064,256]{2,1,0:T(8,128)(2,1)} %pad_maximum_fusion.own), channel_id=1, source_target_pairs={{0,1},{1,0},{2,3},{3,2},{4,5},{5,4},{6,7},{7,6},{8,9},{9,8},{10,11... | collective-permute-start | bytes 12681224 | tf_op jit(solution)/shard_map/ppermute | solution.py:230
  42.1 61.7 %collective-permute-start.3 = (bf16[2064,256]{1,0:T(8,128)(2,1)}, bf16[2064,256]{1,0:T(8,128)(2,1)S(1)}, u32[]{:S(2)}, u32[]{:S(2)}) collective-permute-start(bf16[2064,256]{1,0:T(8,128)(2,1)} %dynamic_update_slice.13), channel_id=1, source_target_pairs={{1,2},{2,1},{3,4},{4,3},{5,6},{6,5},{7,8},{8,7},{9,10},{10,9},{11,... | collective-permute-start | bytes 3170312 | tf_op jit(solution)/shard_map/ppermute | solution.py:228
  45.1 70.2 %collective-permute-start.2 = (bf16[2064,256]{1,0:T(8,128)(2,1)}, bf16[2064,256]{1,0:T(8,128)(2,1)}, u32[]{:S(2)}, u32[]{:S(2)}) collective-permute-start(bf16[2064,256]{1,0:T(8,128)(2,1)} %dynamic_update_slice.12), channel_id=1, source_target_pairs={{1,2},{2,1},{3,4},{4,3},{5,6},{6,5},{7,8},{8,7},{9,10},{10,9},{11,... | collective-permute-start | bytes 3170312 | tf_op jit(solution)/shard_map/ppermute | solution.py:228
  47.7 118.9 %collective-permute-start.1 = (bf16[2064,256]{1,0:T(8,128)(2,1)}, bf16[2064,256]{1,0:T(8,128)(2,1)S(1)}, u32[]{:S(2)}, u32[]{:S(2)}) collective-permute-start(bf16[2064,256]{1,0:T(8,128)(2,1)} %dynamic_update_slice.15), channel_id=1, source_target_pairs={{1,2},{2,1},{3,4},{4,3},{5,6},{6,5},{7,8},{8,7},{9,10},{10,9},{11,... | collective-permute-start | bytes 3170312 | tf_op jit(solution)/shard_map/ppermute | solution.py:228
  50.7 87.2 %collective-permute-start.4 = (bf16[2064,256]{1,0:T(8,128)(2,1)}, bf16[2064,256]{1,0:T(8,128)(2,1)}, u32[]{:S(2)}, u32[]{:S(2)}) collective-permute-start(bf16[2064,256]{1,0:T(8,128)(2,1)} %dynamic_update_slice.14), channel_id=1, source_target_pairs={{1,2},{2,1},{3,4},{4,3},{5,6},{6,5},{7,8},{8,7},{9,10},{10,9},{11,... | collective-permute-start | bytes 3170312 | tf_op jit(solution)/shard_map/ppermute | solution.py:228
  98.9 1.3 copy-start.1
  166.6 1.6 copy-start

commit v2 on v1

v2 whole, which is shorter than its diff:
```python
import functools

import jax
import jax.numpy as jnp
from jax import lax
from jax.experimental import pallas as pl
from jax.experimental.pallas import tpu as pltpu
from jax.sharding import PartitionSpec as P

SUB = 16
STEP = 8
LANES = 128
COLS = 256
REACH = 1024
NEAR_VMEM = 36 * 1024 * 1024
FAR_VMEM = 16 * 1024 * 1024
NT = (((1,), (1,)), ((), ()))


def dot_nt(a, b):
    return lax.dot_general(a, b, NT, preferred_element_type=jnp.float32)


def up_to(value, unit):
    return -(-value // unit) * unit


def tile_of(rows):
    return max(n for n in range(SUB, 705, SUB) if rows % n == 0)


def rows_from(load, start, count):
    skip = start % STEP
    base = pl.multiple_of(start - skip, STEP)
    block = load(base, count + STEP)
    width = block.shape[1]
    block = block.reshape(count // STEP + 1, STEP, width)
    turned = pltpu.roll(block, (STEP - skip) % STEP, 1)
    row = lax.broadcasted_iota(jnp.int32, (count // STEP, STEP, width), 1)
    return jnp.where(row < STEP - skip, turned[:-1], turned[1:]).reshape(count, width)


def clear_margins(buf, rows):
    width = buf.shape[1]
    buf[:REACH, :] = jnp.zeros((REACH, width), buf.dtype)
    buf[REACH + rows :, :] = jnp.zeros((buf.shape[0] - REACH - rows, width), buf.dtype)


def align(source, lead, wide, buf):
    aux, width = source.shape
    rows = aux + SUB
    wide[:SUB, :] = jnp.zeros((SUB, width), jnp.float32)
    wide[SUB + aux :, :] = jnp.zeros((wide.shape[0] - SUB - aux, width), jnp.float32)
    tile = tile_of(aux)

    def widen(i, carry):
        base = pl.multiple_of(i * tile, SUB)
        wide[pl.ds(pl.multiple_of(SUB + base, SUB), tile), :] = source[
            pl.ds(base, tile), :
        ].astype(jnp.float32)
        return carry

    lax.fori_loop(0, aux // tile, widen, 0)
    step = tile_of(rows)

    def move(i, carry):
        base = pl.multiple_of(i * step, SUB)
        moved = rows_from(lambda at, n: wide[pl.ds(at, n), :], SUB - lead + base, step)
        buf[pl.ds(pl.multiple_of(REACH + base, SUB), step), :] = moved.astype(buf.dtype)
        return carry

    lax.fori_loop(0, rows // step, move, 0)


def add_pair(weight, offset, occ, eps_a, eps_b, ft, buf, acc, dens):
    rows, width = acc.shape
    depth = ft.shape[1]
    scale = float(width) ** -0.5
    coulomb = jnp.dot(
        ft[...], buf[pl.ds(offset, depth), :], preferred_element_type=jnp.float32
    )
    amplitude = (coulomb / (occ - eps_a - eps_b)).astype(jnp.bfloat16)
    dens[...] += (weight * scale) * dot_nt(amplitude, amplitude)
    step = tile_of(rows)

    def add(i, carry):
        base = pl.multiple_of(i * step, SUB)
        block = buf[pl.ds(pl.multiple_of(offset + base, SUB), step), :]
        acc[pl.ds(base, step), :] += weight * dot_nt(block, amplitude)
        return carry

    lax.fori_loop(0, rows // step, add, 0)


def add_block(meta, group, t, at, eps_col, eps_row, ft, buf, acc, dens):
    count, shift, occ = meta
    owned = acc.shape[0]
    cols = buf.shape[1]

    def one(s, carry):
        slot = (group * owned + s) * owned + t

        @pl.when(count[slot] != 0)
        def _():
            add_pair(
                count[slot].astype(jnp.float32),
                pl.multiple_of(REACH + shift[slot], SUB),
                occ[slot],
                eps_col[s],
                eps_row[group * owned + t, :, at : at + cols],
                ft.at[s],
                buf,
                acc.at[s],
                dens.at[s],
            )

        return carry

    lax.fori_loop(0, owned, one, 0)


def own_kernel(
    count, shift, occ, lead, eps_col, eps_row, own, acc, dens, ft, bufs, wide
):
    owned, aux, width = own.shape
    rows = aux + SUB
    depth = ft.shape[2]
    acc[...] = jnp.zeros_like(acc)
    dens[...] = jnp.zeros_like(dens)
    for t in range(owned):
        buf = bufs.at[t]
        clear_margins(buf, rows)
        align(own.at[t], lead[t], wide, buf)

        def turn(i, carry):
            at = pl.multiple_of(i * LANES, LANES)
            ft[t, :, pl.ds(at, LANES)] = buf[pl.ds(REACH + at, LANES), :].T
            return carry

        lax.fori_loop(0, depth // LANES, turn, 0)
    for t in range(owned):
        add_block(
            (count, shift, occ), 0, t, 0, eps_col, eps_row, ft, bufs.at[t], acc, dens
        )


def mate_kernel(
    count, shift, occ, lead, eps_col, eps_row, ft, mate, acc_in, dens_in, acc, dens, buf, wide
):
    del acc_in, dens_in
    owned, aux, width = mate.shape
    clear_margins(buf, aux + SUB)
    for t in range(owned):
        align(mate.at[t], lead[owned + t], wide, buf)
        add_block((count, shift, occ), 1, t, 0, eps_col, eps_row, ft, buf, acc, dens)


def far_kernel(
    count, shift, occ, lead, eps_col, eps_row, ft, block, acc_in, dens_in, acc, dens, buf, wide,
    *, t, at,
):
    del acc_in, dens_in
    owned = acc.shape[0]
    aux = block.shape[0]
    clear_margins(buf, aux + SUB)
    align(block, lead[2 * owned + t], wide, buf)
    add_block((count, shift, occ), 2, t, at, eps_col, eps_row, ft, buf, acc, dens)


def last_kernel(
    count, shift, occ, lead, eps_col, eps_row, ft, block, acc_in, dens_in,
    acc, dens, out, dens_out, buf, wide, ready, sem, *, t, at,
):
    far_kernel(
        count, shift, occ, lead, eps_col, eps_row, ft, block, acc_in, dens_in, acc, dens, buf,
        wide, t=t, at=at,
    )
    owned, aux, width = out.shape
    step = tile_of(aux)
    copies = [pltpu.make_async_copy(dens, dens_out, sem.at[owned])]
    copies[0].start()
    for s in range(owned):

        def settle(i, carry):
            base = pl.multiple_of(i * step, SUB)
            rows = rows_from(lambda at, n: acc[s, pl.ds(at, n), :], lead[s] + base, step)
            ready[s, pl.ds(base, step), :] = rows.astype(ready.dtype)
            return carry

        lax.fori_loop(0, aux // step, settle, 0)
        copies.append(pltpu.make_async_copy(ready.at[s], out.at[s], sem.at[s]))
        copies[-1].start()
    for copy in copies:
        copy.wait()


def copy_kernel(source, after, out, sem, *, t, at):
    del after
    copy = pltpu.make_async_copy(source.at[t, :, pl.ds(at, out.shape[1])], out, sem)
    copy.start()
    copy.wait()


def spec(space):
    return pl.BlockSpec(memory_space=space)


def on_device(fitted, fit_start, virt_domain, occ_energy, virt_energy, pair_partner):
    owned, aux, width = fitted.shape
    devices = lax.axis_size("row")
    position = lax.axis_index("row")
    orbitals = fit_start.shape[0]
    pairs = pair_partner.shape[0]
    pairs_here = pairs // devices
    rows = aux + SUB
    depth = up_to(rows, LANES)
    buf_rows = 2 * REACH + depth
    wide_rows = aux + 2 * SUB + STEP
    smem, vmem, anywhere = spec(pltpu.SMEM), spec(pltpu.VMEM), spec(pl.ANY)

    outward = []
    for i in range(devices):
        to = i + 1 if i % 2 else i - 1
        if 0 <= to < devices:
            outward.append((i, to))
    inward = [(i, i ^ 1) for i in range(devices) if i ^ 1 < devices]

    def in_vmem(array):
        return pltpu.with_memory_space_constraint(array, pltpu.VMEM)

    def chunk(t, at, after):
        return pl.pallas_call(
            functools.partial(copy_kernel, t=t, at=at),
            out_shape=jax.ShapeDtypeStruct((aux, COLS), fitted.dtype),
            in_specs=[anywhere] * 2,
            out_specs=anywhere,
            scratch_shapes=[pltpu.SemaphoreType.DMA],
            name=f"chunk_{t}_{at}",
        )(fitted, after)

    places_of = [(t, at) for t in range(owned) for at in range(0, width, COLS)]
    far = [lax.ppermute(fitted[0, :, :COLS], "row", outward)]
    mate = lax.ppermute(fitted, "row", inward)
    for number, (t, at) in enumerate(places_of[1:], 1):
        after = far[number - 2] if number > 1 else fit_start
        far.append(lax.ppermute(chunk(t, at, after), "row", outward))

    side = jnp.where(position % 2 == 1, 1, -1)
    bases = jnp.stack([position, position - side, position + side]) * owned
    places = bases[:, None] + jnp.arange(owned, dtype=jnp.int32)
    inside = jnp.clip(places, 0, orbitals - 1)
    pick = inside[:, :, None] == jnp.arange(orbitals, dtype=jnp.int32)
    starts = jnp.sum(jnp.where(pick, fit_start, 0), axis=-1)
    occs = jnp.sum(jnp.where(pick, occ_energy, 0.0), axis=-1)
    lead = starts % SUB
    aligned = starts - lead
    mine = places[0]
    shift = aligned[0][None, :, None] - aligned[:, None, :]
    occ = occs[0][None, :, None] + occs[:, None, :]
    ordinal = jnp.arange(pairs, dtype=jnp.int32)
    first = (ordinal // pairs_here) * owned + (ordinal % pairs_here) % owned
    is_mine = mine[None, :, None, None]
    is_other = places[:, None, :, None]
    count = jnp.sum(
        ((first == is_mine) & (pair_partner == is_other)).astype(jnp.int32)
        + ((pair_partner == is_mine) & (first == is_other)).astype(jnp.int32),
        axis=-1,
    )
    domains = jnp.stack(
        [lax.dynamic_slice_in_dim(virt_domain, bases[g], owned, 0) for g in range(3)]
    )
    table = jnp.arange(virt_energy.shape[0], dtype=jnp.int32)
    eps = jnp.sum(jnp.where(domains[..., None] == table, virt_energy, 0.0), axis=-1)
    eps_col = eps[0].reshape(owned, width, 1)
    eps_row = eps.reshape(3 * owned, 1, width)
    meta = (count.reshape(-1), shift.reshape(-1), occ.reshape(-1), lead.reshape(-1))
    meta = meta + (eps_col, eps_row)
    meta_specs = [smem] * 4 + [vmem] * 2

    unit = 4 * rows * width * COLS
    acc_shape = pltpu.VMEM((owned, rows, width), jnp.float32)
    dens_shape = pltpu.VMEM((owned, width, width), jnp.float32)
    ft_shape = pltpu.VMEM((owned, width, depth), fitted.dtype)

    def cost(blocks):
        return pl.CostEstimate(
            flops=unit * blocks * owned, bytes_accessed=8 << 20, transcendentals=0
        )

    acc, dens, ft = pl.pallas_call(
        own_kernel,
        out_shape=(acc_shape, dens_shape, ft_shape),
        in_specs=meta_specs + [vmem],
        out_specs=(vmem, vmem, vmem),
        scratch_shapes=[
            pltpu.VMEM((owned, buf_rows, width), fitted.dtype),
            pltpu.VMEM((wide_rows, width), jnp.float32),
        ],
        compiler_params=pltpu.CompilerParams(vmem_limit_bytes=NEAR_VMEM),
        cost_estimate=cost(len(places_of)),
        name="own_pairs",
    )(*meta, fitted)

    first_state = len(meta) + 2
    acc, dens = pl.pallas_call(
        mate_kernel,
        out_shape=(acc_shape, dens_shape),
        in_specs=meta_specs + [vmem] * 4,
        out_specs=(vmem, vmem),
        input_output_aliases={first_state: 0, first_state + 1: 1},
        scratch_shapes=[
            pltpu.VMEM((buf_rows, width), fitted.dtype),
            pltpu.VMEM((wide_rows, width), jnp.float32),
        ],
        compiler_params=pltpu.CompilerParams(vmem_limit_bytes=NEAR_VMEM),
        cost_estimate=cost(len(places_of)),
        name="mate_pairs",
    )(*meta, in_vmem(ft), mate, in_vmem(acc), in_vmem(dens))

    far_scratch = [
        pltpu.VMEM((buf_rows, COLS), fitted.dtype),
        pltpu.VMEM((wide_rows, COLS), jnp.float32),
    ]
    for number, (t, at) in enumerate(places_of[:-1]):
        acc, dens = pl.pallas_call(
            functools.partial(far_kernel, t=t, at=at),
            out_shape=(acc_shape, dens_shape),
            in_specs=meta_specs + [vmem] * 4,
            out_specs=(vmem, vmem),
            input_output_aliases={first_state: 0, first_state + 1: 1},
            scratch_shapes=far_scratch,
            compiler_params=pltpu.CompilerParams(vmem_limit_bytes=FAR_VMEM),
            cost_estimate=cost(1),
            name=f"far_pairs_{number}",
        )(*meta, in_vmem(ft), far[number], in_vmem(acc), in_vmem(dens))

    t, at = places_of[-1]
    _, _, gradient, density = pl.pallas_call(
        functools.partial(last_kernel, t=t, at=at),
        out_shape=(
            acc_shape,
            dens_shape,
            jax.ShapeDtypeStruct(fitted.shape, fitted.dtype),
            jax.ShapeDtypeStruct((owned, width, width), jnp.float32),
        ),
        in_specs=meta_specs + [vmem] * 4,
        out_specs=(vmem, vmem, anywhere, anywhere),
        input_output_aliases={first_state: 0, first_state + 1: 1},
        scratch_shapes=far_scratch
        + [
            pltpu.VMEM((owned, aux, width), fitted.dtype),
            pltpu.SemaphoreType.DMA((owned + 1,)),
        ],
        compiler_params=pltpu.CompilerParams(vmem_limit_bytes=FAR_VMEM),
        cost_estimate=cost(1),
        name="last_pairs",
    )(*meta, in_vmem(ft), far[-1], in_vmem(acc), in_vmem(dens))
    return gradient, density


def solution(mesh):
    placed = (
        P(("parts", "row"), None, None),
        P("parts"),
        P("parts", None),
        P("parts"),
        P("parts"),
        P("parts"),
    )
    return jax.shard_map(
        on_device,
        mesh=mesh,
        in_specs=placed,
        out_specs=(P(("parts", "row"), None, None), P(("parts", "row"), None, None)),
        check_vma=False,
    )
```

time: 182 us -> 182 us (level)
  the two profiles are of different devices: /device:TPU:25 before, /device:TPU:1 now
where the time goes in v2:
time: 182 us; the launch traced here: 180 us
  Pallas kernels  144 us (79%)
  local copies, waits for them, and re-layouts  15.4 us (8%)
  starting transfers between devices  12.4 us (7%)
  between operations  6.52 us (4%)
  other arithmetic  2.08 us (1%)
    pallas_call x3, Pallas kernels, chunk(): pl.pallas_call(functools.partial(copy_kernel, t=t, at=at), out_shape=jax....  98.6 us
    pallas_call x3, Pallas kernels, on_device(): pl.pallas_call(functools.partial(far_kernel, t=t, at=at), out_shape=(acc_...  17 us
    pallas_call x1, Pallas kernels, on_device(): pl.pallas_call(own_kernel, out_shape=(acc_shape, dens_shape, ft_shape), i...  11 us
    unnamed x16, local copies, waits for them, and re-layouts  11 us
    pallas_call x1, Pallas kernels, on_device(): pl.pallas_call(mate_kernel, out_shape=(acc_shape, dens_shape), in_specs=m...  10.7 us
    ppermute x3, starting transfers between devices, on_device(): far.append(lax.ppermute(chunk(t, at, after), 'row', outward))  7.67 us
    pallas_call x1, Pallas kernels, on_device(): pl.pallas_call(functools.partial(last_kernel, t=t, at=at), out_shape=(acc...  6.14 us
    ppermute x1, starting transfers between devices, on_device(): far = [lax.ppermute(fitted[0, :, :COLS], 'row', outward)]  4.63 us
  transfers between devices with their start and end apart: 5, of which 0 were waited for; matrix products, arithmetic and copies ran while one was open for 4% of the time, Pallas kernels for 76%

profile of v2, /device:TPU:1, one launch (start us, length us, event | category | flops | bytes accessed | tf_op | source)
XLA Modules:
  0.0 179.9 jit_solution(8991079603117038103)
XLA Ops:
  0.6 0.1 collective-permute-start.4
  0.8 2.3 %slice_bitcast_fusion = bf16[2048,256]{1,0:T(8,128)(2,1)} fusion(bf16[2,2048,512]{2,1,0:T(8,128)(2,1)} %source.5), kind=kLoop, calls=%fused_computation.2 | loop fusion | bytes 2097152 | tf_op jit(solution)/shard_map/squeeze | solution.py:242
  3.0 4.6 %collective-permute-start.2 = (bf16[2048,256]{1,0:T(8,128)(2,1)}, bf16[2048,256]{1,0:T(8,128)(2,1)}, u32[]{:S(2)}, u32[]{:S(2)}) collective-permute-start(bf16[2048,256]{1,0:T(8,128)(2,1)} %slice_bitcast_fusion), channel_id=1, source_target_pairs={{1,2},{2,1},{3,4},{4,3},{5,6},{6,5},{7,8},{8,7},{9,10},{10,9},{11,... | collective-permute-start | bytes 3145736 | tf_op jit(solution)/shard_map/ppermute | solution.py:242
  7.7 32.9 %chunk_0_256.1 = bf16[2048,256]{1,0:T(8,128)(2,1)} custom-call(bf16[2,2048,512]{2,1,0:T(8,128)(2,1)} %source.5, s32[32]{0:T(128)} %after.1), custom_call_target="tpu_custom_call" | custom-call | tf_op jit(solution)/shard_map/chunk_0_256/pallas_call | solution.py:232
  40.6 1.9 %collective-permute-start = (bf16[2048,256]{1,0:T(8,128)(2,1)}, bf16[2048,256]{1,0:T(8,128)(2,1)}, u32[]{:S(2)}, u32[]{:S(2)}) collective-permute-start(bf16[2048,256]{1,0:T(8,128)(2,1)} %chunk_0_256.1), channel_id=1, source_target_pairs={{1,2},{2,1},{3,4},{4,3},{5,6},{6,5},{7,8},{8,7},{9,10},{10,9},{11,... | collective-permute-start | bytes 3145736 | tf_op jit(solution)/shard_map/ppermute | solution.py:246
  42.5 0.1 add_multiply_fusion
  42.6 0.6 fusion.8
  48.7 0.9 dynamic-slice_bitcast_fusion.2
  49.7 0.2 select_reduce_fusion.2
  49.9 0.2 select_reduce_fusion.1
  50.1 1.0 select_reduce_fusion
  51.2 0.1 broadcast_compare_fusion.3
  51.4 0.2 fusion.1
  51.7 0.1 reduce_sum.41
  51.8 0.2 copy.29.eps_col
  52.0 0.1 add.118.occ
  52.1 0.1 sub.44.shift
  52.1 0.1 reshape.173.count
  52.2 11.0 %own_pairs.1 = (f32[2,2064,512]{2,1,0:T(8,128)S(1)}, f32[2,512,512]{2,1,0:T(8,128)S(1)}, bf16[2,512,2176]{2,1,0:T(8,128)(2,1)S(1)}) custom-call(s32[12]{0:T(128)S(1)} %reshape.173.count, s32[12]{0:T(128)S(1)} %sub.44.shift, f32[12]{0:T(128)S(1)} %add.118.occ, s32[6]{0:T(128)S(1)} %and_select_fusion.lead, f32[2,512,1]{2,1,0:T(8,128)S(1)} %copy.29.eps_col, ...), custom_call_target="tpu_custom_call" | custom-call | flops 8657043456 | bytes 8388608 | tf_op jit(solution)/shard_map/own_pairs/pallas_call | solution.py:290
  63.3 3.2 %copy-done = f32[2,2064,512]{2,1,0:T(8,128)} copy-done((f32[2,2064,512]{2,1,0:T(8,128)}, f32[2,2064,512]{2,1,0:T(8,128)S(1)}, u32[]{:S(2)}) %copy-start) | copy-done | bytes 8454168
  66.6 2.1 %copy-done.2 = bf16[2,512,2176]{2,1,0:T(8,128)(2,1)} copy-done((bf16[2,512,2176]{2,1,0:T(8,128)(2,1)}, bf16[2,512,2176]{2,1,0:T(8,128)(2,1)S(1)}, u32[]{:S(2)}) %copy-start.2) | copy-done | bytes 4456472
  68.6 32.9 %chunk_1_0.1 = bf16[2048,256]{1,0:T(8,128)(2,1)} custom-call(bf16[2,2048,512]{2,1,0:T(8,128)(2,1)} %source.5, bf16[2048,256]{1,0:T(8,128)(2,1)} %collective-permute-done.2.after.block), custom_call_target="tpu_custom_call" | custom-call | tf_op jit(solution)/shard_map/chunk_1_0/pallas_call | solution.py:232
  101.5 1.9 %collective-permute-start.3 = (bf16[2048,256]{1,0:T(8,128)(2,1)}, bf16[2048,256]{1,0:T(8,128)(2,1)}, u32[]{:S(2)}, u32[]{:S(2)}) collective-permute-start(bf16[2048,256]{1,0:T(8,128)(2,1)} %chunk_1_0.1), channel_id=1, source_target_pairs={{1,2},{2,1},{3,4},{4,3},{5,6},{6,5},{7,8},{8,7},{9,10},{10,9},{11,... | collective-permute-start | bytes 3145736 | tf_op jit(solution)/shard_map/ppermute | solution.py:246
  103.5 32.9 %chunk_1_256.1 = bf16[2048,256]{1,0:T(8,128)(2,1)} custom-call(bf16[2,2048,512]{2,1,0:T(8,128)(2,1)} %source.5, bf16[2048,256]{1,0:T(8,128)(2,1)} %collective-permute-done.after.block), custom_call_target="tpu_custom_call" | custom-call | tf_op jit(solution)/shard_map/chunk_1_256/pallas_call | solution.py:232
  136.3 3.8 %collective-permute-start.1 = (bf16[2048,256]{1,0:T(8,128)(2,1)}, bf16[2048,256]{1,0:T(8,128)(2,1)S(1)}, u32[]{:S(2)}, u32[]{:S(2)}) collective-permute-start(bf16[2048,256]{1,0:T(8,128)(2,1)} %chunk_1_256.1), channel_id=1, source_target_pairs={{1,2},{2,1},{3,4},{4,3},{5,6},{6,5},{7,8},{8,7},{9,10},{10,9},{11,... | collective-permute-start | bytes 3145736 | tf_op jit(solution)/shard_map/ppermute | solution.py:246
  140.2 3.4 %copy-done.1 = f32[2,2064,512]{2,1,0:T(8,128)S(1)} copy-done((f32[2,2064,512]{2,1,0:T(8,128)S(1)}, f32[2,2064,512]{2,1,0:T(8,128)}, u32[]{:S(2)}) %copy-start.1) | copy-done | bytes 8454168
  143.6 2.3 %copy-done.3 = bf16[2,512,2176]{2,1,0:T(8,128)(2,1)S(1)} copy-done((bf16[2,512,2176]{2,1,0:T(8,128)(2,1)S(1)}, bf16[2,512,2176]{2,1,0:T(8,128)(2,1)}, u32[]{:S(2)}) %copy-start.3) | copy-done | bytes 4456472
  145.9 10.7 %mate_pairs.1 = (f32[2,2064,512]{2,1,0:T(8,128)S(1)}, f32[2,512,512]{2,1,0:T(8,128)S(1)}) custom-call(s32[12]{0:T(128)S(1)} %reshape.173.count, s32[12]{0:T(128)S(1)} %sub.44.shift, f32[12]{0:T(128)S(1)} %add.118.occ, s32[6]{0:T(128)S(1)} %and_select_fusion.lead, f32[2,512,1]{2,1,0:T(8,128)S(1)} %copy.29.eps_col, ...), custom_call_target="tpu_custom_call", output_to_operand_aliasing={{0}: (8, {}), {1}: (9, {})} | custom-call | flops 8657043456 | bytes 8388608 | tf_op jit(solution)/shard_map/mate_pairs/pallas_call | solution.py:305
  156.5 6.5 %far_pairs_0.1 = (f32[2,2064,512]{2,1,0:T(8,128)S(1)}, f32[2,512,512]{2,1,0:T(8,128)S(1)}) custom-call(s32[12]{0:T(128)S(1)} %reshape.173.count, s32[12]{0:T(128)S(1)} %sub.44.shift, f32[12]{0:T(128)S(1)} %add.118.occ, s32[6]{0:T(128)S(1)} %and_select_fusion.lead, f32[2,512,1]{2,1,0:T(8,128)S(1)} %copy.29.eps_col, ...), custom_call_target="tpu_custom_call", output_to_operand_aliasing={{0}: (8, {}), {1}: (9, {})} | custom-call | flops 2164260864 | bytes 8388608 | tf_op jit(solution)/shard_map/far_pairs_0/pallas_call | solution.py:325
  163.0 6.5 %far_pairs_1.1 = (f32[2,2064,512]{2,1,0:T(8,128)S(1)}, f32[2,512,512]{2,1,0:T(8,128)S(1)}) custom-call(s32[12]{0:T(128)S(1)} %reshape.173.count, s32[12]{0:T(128)S(1)} %sub.44.shift, f32[12]{0:T(128)S(1)} %add.118.occ, s32[6]{0:T(128)S(1)} %and_select_fusion.lead, f32[2,512,1]{2,1,0:T(8,128)S(1)} %copy.29.eps_col, ...), custom_call_target="tpu_custom_call", output_to_operand_aliasing={{0}: (8, {}), {1}: (9, {})} | custom-call | flops 2164260864 | bytes 8388608 | tf_op jit(solution)/shard_map/far_pairs_1/pallas_call | solution.py:325
  169.5 4.1 %far_pairs_2.1 = (f32[2,2064,512]{2,1,0:T(8,128)S(1)}, f32[2,512,512]{2,1,0:T(8,128)S(1)}) custom-call(s32[12]{0:T(128)S(1)} %reshape.173.count, s32[12]{0:T(128)S(1)} %sub.44.shift, f32[12]{0:T(128)S(1)} %add.118.occ, s32[6]{0:T(128)S(1)} %and_select_fusion.lead, f32[2,512,1]{2,1,0:T(8,128)S(1)} %copy.29.eps_col, ...), custom_call_target="tpu_custom_call", output_to_operand_aliasing={{0}: (8, {}), {1}: (9, {})} | custom-call | flops 2164260864 | bytes 8388608 | tf_op jit(solution)/shard_map/far_pairs_2/pallas_call | solution.py:325
  173.6 6.1 %last_pairs.1 = (f32[2,2064,512]{2,1,0:T(8,128)S(1)}, f32[2,512,512]{2,1,0:T(8,128)S(1)}, bf16[2,2048,512]{2,1,0:T(8,128)(2,1)}, f32[2,512,512]{2,1,0:T(8,128)}) custom-call(s32[12]{0:T(128)S(1)} %reshape.173.count, s32[12]{0:T(128)S(1)} %sub.44.shift, f32[12]{0:T(128)S(1)} %add.118.occ, ...), custom_call_target="tpu_custom_call", output_to_operand_aliasing={{0}: (8, {}), {1}: (9, {})} | custom-call | flops 2164260864 | bytes 8388608 | tf_op jit(solution)/shard_map/last_pairs/pallas_call | solution.py:338
  (30 shorter events, 0.4 us)
Async XLA Ops:
  0.6 139.6 %collective-permute-start.4 = (bf16[2,2048,512]{2,1,0:T(8,128)(2,1)}, bf16[2,2048,512]{2,1,0:T(8,128)(2,1)}, u32[]{:S(2)}, u32[]{:S(2)}) collective-permute-start(bf16[2,2048,512]{2,1,0:T(8,128)(2,1)} %source.5), channel_id=1, source_target_pairs={{0,1},{1,0},{2,3},{3,2},{4,5},{5,4},{6,7},{7,6},{8,9},{9,8},{10,11... | collective-permute-start | bytes 12582920 | tf_op jit(solution)/shard_map/ppermute | solution.py:243
  3.0 46.7 %copy-start.5 = (s32[32]{0:T(128)S(1)}, s32[32]{0:T(128)}, u32[]{:S(2)}) copy-start(s32[32]{0:T(128)} %after.1) | copy-start | bytes 388
  3.0 46.9 %copy-start.7 = (f32[32]{0:T(128)S(1)}, f32[32]{0:T(128)}, u32[]{:S(2)}) copy-start(f32[32]{0:T(128)} %param.9) | copy-start | bytes 388
  3.0 47.0 %copy-start.6 = (f32[256]{0:T(256)S(1)}, f32[256]{0:T(256)}, u32[]{:S(2)}) copy-start(f32[256]{0:T(256)} %param.10) | copy-start | bytes 3076
  3.0 48.1 %copy-start.4 = (s32[48]{0:T(128)S(1)}, s32[48]{0:T(128)}, u32[]{:S(2)}) copy-start(s32[48]{0:T(128)} %param.11) | copy-start | bytes 580
  3.0 65.6 %collective-permute-start.2 = (bf16[2048,256]{1,0:T(8,128)(2,1)}, bf16[2048,256]{1,0:T(8,128)(2,1)}, u32[]{:S(2)}, u32[]{:S(2)}) collective-permute-start(bf16[2048,256]{1,0:T(8,128)(2,1)} %slice_bitcast_fusion), channel_id=1, source_target_pairs={{1,2},{2,1},{3,4},{4,3},{5,6},{6,5},{7,8},{8,7},{9,10},{10,9},{11,... | collective-permute-start | bytes 3145736 | tf_op jit(solution)/shard_map/ppermute | solution.py:242
  40.6 62.9 %collective-permute-start = (bf16[2048,256]{1,0:T(8,128)(2,1)}, bf16[2048,256]{1,0:T(8,128)(2,1)}, u32[]{:S(2)}, u32[]{:S(2)}) collective-permute-start(bf16[2048,256]{1,0:T(8,128)(2,1)} %chunk_0_256.1), channel_id=1, source_target_pairs={{1,2},{2,1},{3,4},{4,3},{5,6},{6,5},{7,8},{8,7},{9,10},{10,9},{11,... | collective-permute-start | bytes 3145736 | tf_op jit(solution)/shard_map/ppermute | solution.py:246
  63.3 3.3 %copy-start = (f32[2,2064,512]{2,1,0:T(8,128)}, f32[2,2064,512]{2,1,0:T(8,128)S(1)}, u32[]{:S(2)}) copy-start(f32[2,2064,512]{2,1,0:T(8,128)S(1)} %get-tuple-element.16.acc_in) | copy-start | bytes 25362436
  66.6 2.1 %copy-start.2 = (bf16[2,512,2176]{2,1,0:T(8,128)(2,1)}, bf16[2,512,2176]{2,1,0:T(8,128)(2,1)S(1)}, u32[]{:S(2)}) copy-start(bf16[2,512,2176]{2,1,0:T(8,128)(2,1)S(1)} %get-tuple-element.15.ft) | copy-start | bytes 13369348
  101.5 68.0 %collective-permute-start.3 = (bf16[2048,256]{1,0:T(8,128)(2,1)}, bf16[2048,256]{1,0:T(8,128)(2,1)}, u32[]{:S(2)}, u32[]{:S(2)}) collective-permute-start(bf16[2048,256]{1,0:T(8,128)(2,1)} %chunk_1_0.1), channel_id=1, source_target_pairs={{1,2},{2,1},{3,4},{4,3},{5,6},{6,5},{7,8},{8,7},{9,10},{10,9},{11,... | collective-permute-start | bytes 3145736 | tf_op jit(solution)/shard_map/ppermute | solution.py:246
  136.3 37.3 %collective-permute-start.1 = (bf16[2048,256]{1,0:T(8,128)(2,1)}, bf16[2048,256]{1,0:T(8,128)(2,1)S(1)}, u32[]{:S(2)}, u32[]{:S(2)}) collective-permute-start(bf16[2048,256]{1,0:T(8,128)(2,1)} %chunk_1_256.1), channel_id=1, source_target_pairs={{1,2},{2,1},{3,4},{4,3},{5,6},{6,5},{7,8},{8,7},{9,10},{10,9},{11,... | collective-permute-start | bytes 3145736 | tf_op jit(solution)/shard_map/ppermute | solution.py:246
  140.2 3.4 %copy-start.1 = (f32[2,2064,512]{2,1,0:T(8,128)S(1)}, f32[2,2064,512]{2,1,0:T(8,128)}, u32[]{:S(2)}) copy-start(f32[2,2064,512]{2,1,0:T(8,128)} %copy-done) | copy-start | bytes 25362436
  143.6 2.3 %copy-start.3 = (bf16[2,512,2176]{2,1,0:T(8,128)(2,1)S(1)}, bf16[2,512,2176]{2,1,0:T(8,128)(2,1)}, u32[]{:S(2)}) copy-start(bf16[2,512,2176]{2,1,0:T(8,128)(2,1)} %copy-done.2) | copy-start | bytes 13369348

commit v3 on v2

--- a/solution.py
+++ b/solution.py
@@ -14,6 +14,7 @@
 REACH = 1024
 NEAR_VMEM = 36 * 1024 * 1024
 FAR_VMEM = 16 * 1024 * 1024
+CHUNK_VMEM = 5 * 1024 * 1024
 NT = (((1,), (1,)), ((), ()))
 
 
@@ -120,8 +121,9 @@
 
 
 def own_kernel(
-    count, shift, occ, lead, eps_col, eps_row, own, acc, dens, ft, bufs, wide
+    count, shift, occ, lead, eps_col, eps_row, own, acc, dens, ft, token, bufs, wide
 ):
+    token[...] = jnp.zeros_like(token)
     owned, aux, width = own.shape
     rows = aux + SUB
     depth = ft.shape[2]
@@ -145,9 +147,11 @@
 
 
 def mate_kernel(
-    count, shift, occ, lead, eps_col, eps_row, ft, mate, acc_in, dens_in, acc, dens, buf, wide
+    count, shift, occ, lead, eps_col, eps_row, ft, mate, acc_in, dens_in, after,
+    acc, dens, token, buf, wide,
 ):
-    del acc_in, dens_in
+    del acc_in, dens_in, after
+    token[...] = jnp.zeros_like(token)
     owned, aux, width = mate.shape
     clear_margins(buf, aux + SUB)
     for t in range(owned):
@@ -156,10 +160,11 @@
 
 
 def far_kernel(
-    count, shift, occ, lead, eps_col, eps_row, ft, block, acc_in, dens_in, acc, dens, buf, wide,
-    *, t, at,
+    count, shift, occ, lead, eps_col, eps_row, ft, block, acc_in, dens_in, after,
+    acc, dens, token, buf, wide, *, t, at,
 ):
-    del acc_in, dens_in
+    del acc_in, dens_in, after
+    token[...] = jnp.zeros_like(token)
     owned = acc.shape[0]
     aux = block.shape[0]
     clear_margins(buf, aux + SUB)
@@ -168,12 +173,12 @@
 
 
 def last_kernel(
-    count, shift, occ, lead, eps_col, eps_row, ft, block, acc_in, dens_in,
-    acc, dens, out, dens_out, buf, wide, ready, sem, *, t, at,
+    count, shift, occ, lead, eps_col, eps_row, ft, block, acc_in, dens_in, after,
+    acc, dens, token, out, dens_out, buf, wide, ready, sem, *, t, at,
 ):
     far_kernel(
-        count, shift, occ, lead, eps_col, eps_row, ft, block, acc_in, dens_in, acc, dens, buf,
-        wide, t=t, at=at,
+        count, shift, occ, lead, eps_col, eps_row, ft, block, acc_in, dens_in, after,
+        acc, dens, token, buf, wide, t=t, at=at,
     )
     owned, aux, width = out.shape
     step = tile_of(aux)
@@ -194,11 +199,8 @@
         copy.wait()
 
 
-def copy_kernel(source, after, out, sem, *, t, at):
-    del after
-    copy = pltpu.make_async_copy(source.at[t, :, pl.ds(at, out.shape[1])], out, sem)
-    copy.start()
-    copy.wait()
+def copy_kernel(source, *refs):
+    refs[-1][...] = source[0]
 
 
 def spec(space):
@@ -225,25 +227,30 @@
             outward.append((i, to))
     inward = [(i, i ^ 1) for i in range(devices) if i ^ 1 < devices]
 
+    def in_hbm(array):
+        return pltpu.with_memory_space_constraint(array, pltpu.HBM)
+
     def in_vmem(array):
         return pltpu.with_memory_space_constraint(array, pltpu.VMEM)
 
-    def chunk(t, at, after):
+    def chunk(t, at, *after):
         return pl.pallas_call(
-            functools.partial(copy_kernel, t=t, at=at),
+            copy_kernel,
+            grid=(1,),
             out_shape=jax.ShapeDtypeStruct((aux, COLS), fitted.dtype),
-            in_specs=[anywhere] * 2,
-            out_specs=anywhere,
-            scratch_shapes=[pltpu.SemaphoreType.DMA],
+            in_specs=[pl.BlockSpec((1, aux, COLS), lambda i: (t, 0, at // COLS))]
+            + [anywhere] * len(after),
+            out_specs=pl.BlockSpec((aux, COLS), lambda i: (0, 0)),
+            compiler_params=pltpu.CompilerParams(vmem_limit_bytes=CHUNK_VMEM),
             name=f"chunk_{t}_{at}",
-        )(fitted, after)
+        )(in_hbm(fitted), *after)
 
     places_of = [(t, at) for t in range(owned) for at in range(0, width, COLS)]
-    far = [lax.ppermute(fitted[0, :, :COLS], "row", outward)]
+    sent = [chunk(*places_of[0])]
+    far = [lax.ppermute(sent[0], "row", outward)]
     mate = lax.ppermute(fitted, "row", inward)
-    for number, (t, at) in enumerate(places_of[1:], 1):
-        after = far[number - 2] if number > 1 else fit_start
-        far.append(lax.ppermute(chunk(t, at, after), "row", outward))
+    sent.append(chunk(*places_of[1], sent[0]))
+    far.append(lax.ppermute(sent[1], "row", outward))
 
     side = jnp.where(position % 2 == 1, 1, -1)
     bases = jnp.stack([position, position - side, position + side]) * owned
@@ -287,11 +294,12 @@
             flops=unit * blocks * owned, bytes_accessed=8 << 20, transcendentals=0
         )
 
-    acc, dens, ft = pl.pallas_call(
+    token_shape = jax.ShapeDtypeStruct((8, LANES), jnp.int32)
+    acc, dens, ft, token = pl.pallas_call(
         own_kernel,
-        out_shape=(acc_shape, dens_shape, ft_shape),
+        out_shape=(acc_shape, dens_shape, ft_shape, token_shape),
         in_specs=meta_specs + [vmem],
-        out_specs=(vmem, vmem, vmem),
+        out_specs=(vmem,) * 4,
         scratch_shapes=[
             pltpu.VMEM((owned, buf_rows, width), fitted.dtype),
             pltpu.VMEM((wide_rows, width), jnp.float32),
@@ -299,62 +307,52 @@
         compiler_params=pltpu.CompilerParams(vmem_limit_bytes=NEAR_VMEM),
         cost_estimate=cost(len(places_of)),
         name="own_pairs",
-    )(*meta, fitted)
-
-    first_state = len(meta) + 2
-    acc, dens = pl.pallas_call(
-        mate_kernel,
-        out_shape=(acc_shape, dens_shape),
-        in_specs=meta_specs + [vmem] * 4,
-        out_specs=(vmem, vmem),
-        input_output_aliases={first_state: 0, first_state + 1: 1},
-        scratch_shapes=[
-            pltpu.VMEM((buf_rows, width), fitted.dtype),
-            pltpu.VMEM((wide_rows, width), jnp.float32),
-        ],
-        compiler_params=pltpu.CompilerParams(vmem_limit_bytes=NEAR_VMEM),
-        cost_estimate=cost(len(places_of)),
-        name="mate_pairs",
-    )(*meta, in_vmem(ft), mate, in_vmem(acc), in_vmem(dens))
-
-    far_scratch = [
-        pltpu.VMEM((buf_rows, COLS), fitted.dtype),
-        pltpu.VMEM((wide_rows, COLS), jnp.float32),
-    ]
+    )(*meta, in_hbm(fitted))
+
+    def add_pairs(kernel, block, acc, dens, after, cols, limit, blocks, name, outs=(), scratch=()):
+        first_state = len(meta) + 2
+        return pl.pallas_call(
+            kernel,
+            out_shape=(acc_shape, dens_shape, token_shape, *outs),
+            in_specs=meta_specs + [vmem] * 4 + [anywhere],
+            out_specs=(vmem,) * 3 + (anywhere,) * len(outs),
+            input_output_aliases={first_state: 0, first_state + 1: 1},
+            scratch_shapes=[
+                pltpu.VMEM((buf_rows, cols), fitted.dtype),
+                pltpu.VMEM((wide_rows, cols), jnp.float32),
+                *scratch,
+            ],
+            compiler_params=pltpu.CompilerParams(vmem_limit_bytes=limit),
+            cost_estimate=cost(blocks),
+            name=name,
+        )(*meta, in_vmem(ft), block, in_vmem(acc), in_vmem(dens), after)
+
+    acc, dens, token = add_pairs(
+        mate_kernel, mate, acc, dens, token, width, NEAR_VMEM, len(places_of), "mate_pairs"
+    )
+    last = len(places_of) - 1
     for number, (t, at) in enumerate(places_of[:-1]):
-        acc, dens = pl.pallas_call(
+        if number + 2 <= last:
+            sent.append(chunk(*places_of[number + 2], far[number], token))
+            far.append(lax.ppermute(sent[-1], "row", outward))
+            token = sent[-1]
+        acc, dens, token = add_pairs(
             functools.partial(far_kernel, t=t, at=at),
-            out_shape=(acc_shape, dens_shape),
-            in_specs=meta_specs + [vmem] * 4,
-            out_specs=(vmem, vmem),
-            input_output_aliases={first_state: 0, first_state + 1: 1},
-            scratch_shapes=far_scratch,
-            compiler_params=pltpu.CompilerParams(vmem_limit_bytes=FAR_VMEM),
-            cost_estimate=cost(1),
-            name=f"far_pairs_{number}",
-        )(*meta, in_vmem(ft), far[number], in_vmem(acc), in_vmem(dens))
-
+            far[number], acc, dens, token, COLS, FAR_VMEM, 1, f"far_pairs_{number}",
+        )
     t, at = places_of[-1]
-    _, _, gradient, density = pl.pallas_call(
+    *_, gradient, density = add_pairs(
         functools.partial(last_kernel, t=t, at=at),
-        out_shape=(
-            acc_shape,
-            dens_shape,
+        far[-1], acc, dens, token, COLS, FAR_VMEM, 1, "last_pairs",
+        outs=(
             jax.ShapeDtypeStruct(fitted.shape, fitted.dtype),
             jax.ShapeDtypeStruct((owned, width, width), jnp.float32),
         ),
-        in_specs=meta_specs + [vmem] * 4,
-        out_specs=(vmem, vmem, anywhere, anywhere),
-        input_output_aliases={first_state: 0, first_state + 1: 1},
-        scratch_shapes=far_scratch
-        + [
+        scratch=(
             pltpu.VMEM((owned, aux, width), fitted.dtype),
             pltpu.SemaphoreType.DMA((owned + 1,)),
-        ],
-        compiler_params=pltpu.CompilerParams(vmem_limit_bytes=FAR_VMEM),
-        cost_estimate=cost(1),
-        name="last_pairs",
-    )(*meta, in_vmem(ft), far[-1], in_vmem(acc), in_vmem(dens))
+        ),
+    )
     return gradient, density
 
 

time: 182 us -> 107 us (0.59)
  the two profiles are of different devices: /device:TPU:1 before, /device:TPU:9 now
where the time goes in v3:
time: 107 us; the launch traced here: 106 us
  Pallas kernels  49.5 us (46%)
  waiting for transfers between devices  30.9 us (29%)
  starting transfers between devices  14.4 us (13%)
  between operations  6.55 us (6%)
  local copies, waits for them, and re-layouts  2.17 us (2%)
  other arithmetic  2.09 us (2%)
    ppermute x2, waiting for transfers between devices, on_device(): far.append(lax.ppermute(sent[-1], 'row', outward))  30.7 us
    pallas_call x5, Pallas kernels, add_pairs(): pl.pallas_call(kernel, out_shape=(acc_shape, dens_shape, token_shape, *ou...  24.3 us
    pallas_call x1, Pallas kernels, on_device(): pl.pallas_call(own_kernel, out_shape=(acc_shape, dens_shape, ft_shape, to...  18.1 us
    ppermute x2, starting transfers between devices, on_device(): far.append(lax.ppermute(sent[-1], 'row', outward))  7.98 us
    pallas_call x4, Pallas kernels, chunk(): pl.pallas_call(copy_kernel, grid=(1,), out_shape=jax.ShapeDtypeStruct((au...  7.12 us
    ppermute x1, starting transfers between devices, on_device(): far = [lax.ppermute(sent[0], 'row', outward)]  3.18 us
    ppermute x1, starting transfers between devices, on_device(): far.append(lax.ppermute(sent[1], 'row', outward))  2.5 us
  transfers between devices with their start and end apart: 5, of which 3 were waited for; matrix products, arithmetic and copies ran while one was open for 4% of the time, Pallas kernels for 41%

profile of v3, /device:TPU:9, one launch (start us, length us, event | category | flops | bytes accessed | tf_op | source)
XLA Modules:
  0.0 105.6 jit_solution(6235611949452683028)
XLA Ops:
  0.6 0.7 collective-permute-start.2
  1.4 2.3 %chunk_0_0.1.refs_0_ = bf16[2048,256]{1,0:T(8,128)(2,1)} custom-call(bf16[2,2048,512]{2,1,0:T(8,128)(2,1)} %source.7), custom_call_target="tpu_custom_call" | custom-call | tf_op jit(solution)/shard_map/chunk_0_0/pallas_call | solution.py:237
  3.6 3.2 %collective-permute-start.1 = (bf16[2048,256]{1,0:T(8,128)(2,1)}, bf16[2048,256]{1,0:T(8,128)(2,1)S(1)}, u32[]{:S(2)}, u32[]{:S(2)}) collective-permute-start(bf16[2048,256]{1,0:T(8,128)(2,1)} %chunk_0_0.1.refs_0_), channel_id=1, source_target_pairs={{1,2},{2,1},{3,4},{4,3},{5,6},{6,5},{7,8},{8,7},{9,10},{10,9},{11,... | collective-permute-start | bytes 3145736 | tf_op jit(solution)/shard_map/ppermute | solution.py:250
  6.8 2.3 %chunk_0_256.1 = bf16[2048,256]{1,0:T(8,128)(2,1)} custom-call(bf16[2,2048,512]{2,1,0:T(8,128)(2,1)} %source.7, bf16[2048,256]{1,0:T(8,128)(2,1)} %chunk_0_0.1.refs_0_), custom_call_target="tpu_custom_call" | custom-call | tf_op jit(solution)/shard_map/chunk_0_256/pallas_call | solution.py:237
  9.1 2.5 %collective-permute-start = (bf16[2048,256]{1,0:T(8,128)(2,1)}, bf16[2048,256]{1,0:T(8,128)(2,1)S(1)}, u32[]{:S(2)}, u32[]{:S(2)}) collective-permute-start(bf16[2048,256]{1,0:T(8,128)(2,1)} %chunk_0_256.1), channel_id=1, source_target_pairs={{1,2},{2,1},{3,4},{4,3},{5,6},{6,5},{7,8},{8,7},{9,10},{10,9},{11,... | collective-permute-start | bytes 3145736 | tf_op jit(solution)/shard_map/ppermute | solution.py:253
  11.6 0.1 add_multiply_fusion
  11.7 0.7 fusion.8
  16.2 0.1 broadcast_compare_fusion.1
  16.3 0.2 fusion.1
  16.5 0.1 reshape.173.count
  16.6 0.2 select_reduce_fusion.2
  16.8 0.1 reduce_sum.41
  17.0 0.1 sub.44.shift
  17.1 0.2 select_reduce_fusion.1
  17.2 0.1 broadcast_add_fusion
  17.3 0.1 add.118.occ
  19.3 0.9 dynamic-slice_bitcast_fusion.2
  20.2 1.0 select_reduce_fusion
  21.3 0.2 copy.29.eps_col
  21.5 18.1 %own_pairs.1 = (f32[2,2064,512]{2,1,0:T(8,128)S(1)}, f32[2,512,512]{2,1,0:T(8,128)S(1)}, bf16[2,512,2176]{2,1,0:T(8,128)(2,1)S(1)}, s32[8,128]{1,0:T(8,128)S(1)}) custom-call(s32[12]{0:T(128)S(1)} %reshape.173.count, s32[12]{0:T(128)S(1)} %sub.44.shift, f32[12]{0:T(128)S(1)} %add.118.occ, s32[6]{0:T(128)S(1)} %and_select_fusion.lead, ...), custom_call_target="tpu_custom_call" | custom-call | flops 8657043456 | bytes 8388608 | tf_op jit(solution)/shard_map/own_pairs/pallas_call | solution.py:298
  39.7 7.3 %mate_pairs.1 = (f32[2,2064,512]{2,1,0:T(8,128)S(1)}, f32[2,512,512]{2,1,0:T(8,128)S(1)}, s32[8,128]{1,0:T(8,128)S(1)}) custom-call(s32[12]{0:T(128)S(1)} %reshape.173.count, s32[12]{0:T(128)S(1)} %sub.44.shift, f32[12]{0:T(128)S(1)} %add.118.occ, s32[6]{0:T(128)S(1)} %and_select_fusion.lead, ...), custom_call_target="tpu_custom_call", output_to_operand_aliasing={{0}: (8, {}), {1}: (9, {})} | custom-call | flops 8657043456 | bytes 8388608 | tf_op jit(solution)/shard_map/mate_pairs/pallas_call | solution.py:314
  47.0 1.3 %chunk_1_0.1.after = bf16[2048,256]{1,0:T(8,128)(2,1)S(1)} custom-call(bf16[2,2048,512]{2,1,0:T(8,128)(2,1)} %source.7, bf16[2048,256]{1,0:T(8,128)(2,1)S(1)} %collective-permute-done.1.refs_0_.block, s32[8,128]{1,0:T(8,128)S(1)} %get-tuple-element.26.refs_1_), custom_call_target="tpu_custom_call" | custom-call | tf_op jit(solution)/shard_map/chunk_1_0/pallas_call | solution.py:237
  48.3 1.9 %collective-permute-start.4 = (bf16[2048,256]{1,0:T(8,128)(2,1)S(1)}, bf16[2048,256]{1,0:T(8,128)(2,1)S(1)}, u32[]{:S(2)}, u32[]{:S(2)}) collective-permute-start(bf16[2048,256]{1,0:T(8,128)(2,1)S(1)} %chunk_1_0.1.after), channel_id=1, source_target_pairs={{1,2},{2,1},{3,4},{4,3},{5,6},{6,5},{7,8},{8,7},{9,10},{10,9},{11,... | collective-permute-start | bytes 3145736 | tf_op jit(solution)/shard_map/ppermute | solution.py:337
  50.2 3.4 %far_pairs_0.1 = (f32[2,2064,512]{2,1,0:T(8,128)S(1)}, f32[2,512,512]{2,1,0:T(8,128)S(1)}, s32[8,128]{1,0:T(8,128)S(1)}) custom-call(s32[12]{0:T(128)S(1)} %reshape.173.count, s32[12]{0:T(128)S(1)} %sub.44.shift, f32[12]{0:T(128)S(1)} %add.118.occ, s32[6]{0:T(128)S(1)} %and_select_fusion.lead, ...), custom_call_target="tpu_custom_call", output_to_operand_aliasing={{0}: (8, {}), {1}: (9, {})} | custom-call | flops 2164260864 | bytes 8388608 | tf_op jit(solution)/shard_map/far_pairs_0/pallas_call | solution.py:314
  53.7 0.2 collective-permute-done.refs_0_.block
  53.8 1.3 %chunk_1_256.1.after = bf16[2048,256]{1,0:T(8,128)(2,1)S(1)} custom-call(bf16[2,2048,512]{2,1,0:T(8,128)(2,1)} %source.7, bf16[2048,256]{1,0:T(8,128)(2,1)S(1)} %collective-permute-done.refs_0_.block, s32[8,128]{1,0:T(8,128)S(1)} %get-tuple-element.27.refs_1_), custom_call_target="tpu_custom_call" | custom-call | tf_op jit(solution)/shard_map/chunk_1_256/pallas_call | solution.py:237
  55.1 6.1 %collective-permute-start.3 = (bf16[2048,256]{1,0:T(8,128)(2,1)S(1)}, bf16[2048,256]{1,0:T(8,128)(2,1)S(1)}, u32[]{:S(2)}, u32[]{:S(2)}) collective-permute-start(bf16[2048,256]{1,0:T(8,128)(2,1)S(1)} %chunk_1_256.1.after), channel_id=1, source_target_pairs={{1,2},{2,1},{3,4},{4,3},{5,6},{6,5},{7,8},{8,7},{9,10},{10,9},{11,... | collective-permute-start | bytes 3145736 | tf_op jit(solution)/shard_map/ppermute | solution.py:337
  61.2 3.4 %far_pairs_1.1 = (f32[2,2064,512]{2,1,0:T(8,128)S(1)}, f32[2,512,512]{2,1,0:T(8,128)S(1)}, s32[8,128]{1,0:T(8,128)S(1)}) custom-call(s32[12]{0:T(128)S(1)} %reshape.173.count, s32[12]{0:T(128)S(1)} %sub.44.shift, f32[12]{0:T(128)S(1)} %add.118.occ, s32[6]{0:T(128)S(1)} %and_select_fusion.lead, ...), custom_call_target="tpu_custom_call", output_to_operand_aliasing={{0}: (8, {}), {1}: (9, {})} | custom-call | flops 2164260864 | bytes 8388608 | tf_op jit(solution)/shard_map/far_pairs_1/pallas_call | solution.py:314
  64.6 22.9 %collective-permute-done.4.block = bf16[2048,256]{1,0:T(8,128)(2,1)S(1)} collective-permute-done((bf16[2048,256]{1,0:T(8,128)(2,1)S(1)}, bf16[2048,256]{1,0:T(8,128)(2,1)S(1)}, u32[]{:S(2)}, u32[]{:S(2)}) %collective-permute-start.4) | collective-permute-done | bytes 1048608 | tf_op jit(solution)/shard_map/ppermute | solution.py:337
  87.5 3.4 %far_pairs_2.1 = (f32[2,2064,512]{2,1,0:T(8,128)S(1)}, f32[2,512,512]{2,1,0:T(8,128)S(1)}, s32[8,128]{1,0:T(8,128)S(1)}) custom-call(s32[12]{0:T(128)S(1)} %reshape.173.count, s32[12]{0:T(128)S(1)} %sub.44.shift, f32[12]{0:T(128)S(1)} %add.118.occ, s32[6]{0:T(128)S(1)} %and_select_fusion.lead, ...), custom_call_target="tpu_custom_call", output_to_operand_aliasing={{0}: (8, {}), {1}: (9, {})} | custom-call | flops 2164260864 | bytes 8388608 | tf_op jit(solution)/shard_map/far_pairs_2/pallas_call | solution.py:314
  90.9 7.8 %collective-permute-done.3.block = bf16[2048,256]{1,0:T(8,128)(2,1)S(1)} collective-permute-done((bf16[2048,256]{1,0:T(8,128)(2,1)S(1)}, bf16[2048,256]{1,0:T(8,128)(2,1)S(1)}, u32[]{:S(2)}, u32[]{:S(2)}) %collective-permute-start.3) | collective-permute-done | bytes 1048608 | tf_op jit(solution)/shard_map/ppermute | solution.py:337
  98.7 6.7 %last_pairs.1 = (f32[2,2064,512]{2,1,0:T(8,128)S(1)}, f32[2,512,512]{2,1,0:T(8,128)S(1)}, s32[8,128]{1,0:T(8,128)}, bf16[2,2048,512]{2,1,0:T(8,128)(2,1)}, f32[2,512,512]{2,1,0:T(8,128)}) custom-call(s32[12]{0:T(128)S(1)} %reshape.173.count, s32[12]{0:T(128)S(1)} %sub.44.shift, f32[12]{0:T(128)S(1)} %add.118.occ, ...), custom_call_target="tpu_custom_call", output_to_operand_aliasing={{0}: (8, {}), {1}: (9, {})} | custom-call | flops 2164260864 | bytes 8388608 | tf_op jit(solution)/shard_map/last_pairs/pallas_call | solution.py:314
  (22 shorter events, 0.3 us)
Async XLA Ops:
  0.6 39.0 %collective-permute-start.2 = (bf16[2,2048,512]{2,1,0:T(8,128)(2,1)}, bf16[2,2048,512]{2,1,0:T(8,128)(2,1)}, u32[]{:S(2)}, u32[]{:S(2)}) collective-permute-start(bf16[2,2048,512]{2,1,0:T(8,128)(2,1)} %source.7), channel_id=1, source_target_pairs={{0,1},{1,0},{2,3},{3,2},{4,5},{5,4},{6,7},{7,6},{8,9},{9,8},{10,11... | collective-permute-start | bytes 12582920 | tf_op jit(solution)/shard_map/ppermute | solution.py:251
  3.6 12.5 %copy-start = (s32[48]{0:T(128)S(1)}, s32[48]{0:T(128)}, u32[]{:S(2)}) copy-start(s32[48]{0:T(128)} %param.11) | copy-start | bytes 580
  3.6 13.0 %copy-start.2 = (s32[32]{0:T(128)S(1)}, s32[32]{0:T(128)}, u32[]{:S(2)}) copy-start(s32[32]{0:T(128)} %param.7) | copy-start | bytes 388
  3.6 13.4 %copy-start.3 = (f32[32]{0:T(128)S(1)}, f32[32]{0:T(128)}, u32[]{:S(2)}) copy-start(f32[32]{0:T(128)} %param.9) | copy-start | bytes 388
  3.6 16.5 %copy-start.1 = (f32[256]{0:T(256)S(1)}, f32[256]{0:T(256)}, u32[]{:S(2)}) copy-start(f32[256]{0:T(256)} %param.10) | copy-start | bytes 3076
  3.6 43.3 %collective-permute-start.1 = (bf16[2048,256]{1,0:T(8,128)(2,1)}, bf16[2048,256]{1,0:T(8,128)(2,1)S(1)}, u32[]{:S(2)}, u32[]{:S(2)}) collective-permute-start(bf16[2048,256]{1,0:T(8,128)(2,1)} %chunk_0_0.1.refs_0_), channel_id=1, source_target_pairs={{1,2},{2,1},{3,4},{4,3},{5,6},{6,5},{7,8},{8,7},{9,10},{10,9},{11,... | collective-permute-start | bytes 3145736 | tf_op jit(solution)/shard_map/ppermute | solution.py:250
  9.1 44.7 %collective-permute-start = (bf16[2048,256]{1,0:T(8,128)(2,1)}, bf16[2048,256]{1,0:T(8,128)(2,1)S(1)}, u32[]{:S(2)}, u32[]{:S(2)}) collective-permute-start(bf16[2048,256]{1,0:T(8,128)(2,1)} %chunk_0_256.1), channel_id=1, source_target_pairs={{1,2},{2,1},{3,4},{4,3},{5,6},{6,5},{7,8},{8,7},{9,10},{10,9},{11,... | collective-permute-start | bytes 3145736 | tf_op jit(solution)/shard_map/ppermute | solution.py:253
  48.3 39.2 %collective-permute-start.4 = (bf16[2048,256]{1,0:T(8,128)(2,1)S(1)}, bf16[2048,256]{1,0:T(8,128)(2,1)S(1)}, u32[]{:S(2)}, u32[]{:S(2)}) collective-permute-start(bf16[2048,256]{1,0:T(8,128)(2,1)S(1)} %chunk_1_0.1.after), channel_id=1, source_target_pairs={{1,2},{2,1},{3,4},{4,3},{5,6},{6,5},{7,8},{8,7},{9,10},{10,9},{11,... | collective-permute-start | bytes 3145736 | tf_op jit(solution)/shard_map/ppermute | solution.py:337
  55.1 43.6 %collective-permute-start.3 = (bf16[2048,256]{1,0:T(8,128)(2,1)S(1)}, bf16[2048,256]{1,0:T(8,128)(2,1)S(1)}, u32[]{:S(2)}, u32[]{:S(2)}) collective-permute-start(bf16[2048,256]{1,0:T(8,128)(2,1)S(1)} %chunk_1_256.1.after), channel_id=1, source_target_pairs={{1,2},{2,1},{3,4},{4,3},{5,6},{6,5},{7,8},{8,7},{9,10},{10,9},{11,... | collective-permute-start | bytes 3145736 | tf_op jit(solution)/shard_map/ppermute | solution.py:337
